TPU v7x, 128 devices: a whole 4x4x4 slice. The times are simulated.
128 devices in a mesh: ctx: 16 (over y_hi, z, core), dp: 8 (over x, y_lo).
Axes of the slice: x: 4, y: 4 (y_hi: 2, y_lo: 2; y = y_hi * 2 + y_lo), z: 4, core: 2. Of those that a mesh axis runs over, the one named last changes fastest.
Arguments:
- queries: bfloat16 [8192, 24576], P('ctx', 'dp'), may hold values from -170 to 170, as said below
- latent_cache: bfloat16 [8192, 576], P(('ctx', 'dp')), may hold values from -6 to 6
- doc_ids: int32 [8192], P('ctx'), may hold values from 0 to 15, never falling along the last dimension, each value on 1 to 1024 neighbouring positions
- w_key: bfloat16 [512, 16384], P(None, 'dp'), may hold values from -0.25 to 0.25
- w_value: bfloat16 [512, 16384], P(None, 'dp'), may hold values from -0.25 to 0.25
Outputs:
- attended: bfloat16 [8192, 16384], P('ctx', 'dp')
Inputs may be any that keep to these rules, and one draw needn't show every extreme that they name: doc_ids never fall along the sequence; every document holds 1 to 1024 consecutive tokens and some document holds exactly 1024. `queries`: finite values.
All inputs are finite; a program needn't handle non-finite values.
Results may differ from a plain program's by a relative error of at most 0.014.
Values may be sent and summed in bfloat16 or wider, within the bound.
A program may use at most 192 MiB of HBM per device.

v0:
```python
import math

import jax
import jax.numpy as jnp
from jax import lax
from jax.sharding import PartitionSpec as P

LATENT = 512
ROPE = 64
POSITION_FREE = 128
VDIM = 128
WINDOW = 3


NEG_FILL = -1e30


def shifted(value, axis, steps):
    count = lax.axis_size(axis)
    initial, last = (max(0, -steps), min(count, count - steps))
    return lax.ppermute(value, axis, [(source, source + steps) for source in range(initial, last)])


def passed_along(block, axis, distance):
    devices = range(lax.axis_size(axis))
    route = [((i - distance) % len(devices), i) for i in devices]
    return lax.ppermute(block, axis, route)


def expand_block(latent_block, w_key, w_value):
    row_count = latent_block.shape[0]
    local_heads = w_key.shape[1] // POSITION_FREE
    latent = latent_block[:, :LATENT]
    key_rows = jnp.dot(latent, w_key, preferred_element_type=jnp.float32).astype(jnp.bfloat16)
    value_rows = jnp.dot(latent, w_value, preferred_element_type=jnp.float32).astype(jnp.bfloat16)
    return (
        key_rows.reshape(row_count, local_heads, POSITION_FREE),
        value_rows.reshape(row_count, local_heads, VDIM),
        latent_block[:, LATENT:],
    )


def tile_visible(query_seg, key_seg, query_block, key_block, row_count):
    offsets = jnp.arange(row_count, dtype=jnp.int32)
    query_pos = query_block * row_count + offsets
    key_pos = key_block * row_count + offsets
    same_doc = query_seg[:, None] == key_seg[None, :]
    causal = key_pos[None, :] <= query_pos[:, None]
    inside = key_pos[None, :] >= 0
    return same_doc & causal & inside


def attend(carry_state, query_heads, key_rows, value_rows, rope_keys, visible):
    row_peak, weight_sum, accumulated = carry_state
    score_scale = 1.0 / math.sqrt(POSITION_FREE + ROPE)
    logit_scores = jnp.einsum(
        "thd,khd->thk",
        query_heads[..., :POSITION_FREE],
        key_rows,
        preferred_element_type=jnp.float32,
    )
    logit_scores = logit_scores + jnp.einsum(
        "thd,kd->thk",
        query_heads[..., POSITION_FREE:],
        rope_keys,
        preferred_element_type=jnp.float32,
    )
    logit_scores = logit_scores * score_scale
    wide_mask = visible[:, None, :]
    logit_scores = jnp.where(wide_mask, logit_scores, NEG_FILL)
    new_peak = jnp.maximum(row_peak, jnp.max(logit_scores, axis=2))
    softmax_weights = jnp.where(wide_mask, jnp.exp(logit_scores - new_peak[..., None]), 0.0)
    factor = jnp.exp(row_peak - new_peak)
    weight_sum = weight_sum * factor + jnp.sum(softmax_weights, axis=2)
    accumulated = accumulated * factor[..., None] + jnp.einsum(
        "thk,khd->thd",
        softmax_weights.astype(jnp.bfloat16),
        value_rows,
        preferred_element_type=jnp.float32,
    )
    return (new_peak, weight_sum, accumulated)


def run_tile(carry_state, query_heads, key_rows, value_rows, rope_keys, visible):
    return attend(carry_state, query_heads, key_rows, value_rows, rope_keys, visible)


def on_device(queries, latent_cache, doc_ids, w_key, w_value):
    row_count = queries.shape[0]
    local_heads = w_key.shape[1] // POSITION_FREE
    cycle_size = lax.axis_size("ctx")
    cycle_place = lax.axis_index("ctx")
    latent_block = lax.all_gather(latent_cache, "dp", axis=0, tiled=True)
    initial = (
        jnp.full((row_count, local_heads), NEG_FILL, jnp.float32),
        jnp.zeros((row_count, local_heads), jnp.float32),
        jnp.zeros((row_count, local_heads, VDIM), jnp.float32),
    )
    key_rows, value_rows, rope_keys = expand_block(latent_block, w_key, w_value)
    carried = queries
    carried_docs = doc_ids
    carry_state = initial
    for cycle_step in range(WINDOW):
        if cycle_step > 0:
            flat_state = (
                carry_state[0],
                carry_state[1],
                carry_state[2].reshape(row_count, local_heads * VDIM),
            )
            carried = shifted(carried, "ctx", -1)
            carried_docs = shifted(carried_docs, "ctx", -1)
            moved = passed_along((flat_state[0], flat_state[1], flat_state[2]), "ctx", -1)
            carry_state = (moved[0], moved[1], moved[2].reshape(row_count, local_heads, VDIM))
        query_block = (cycle_place + cycle_step) % cycle_size
        visible = tile_visible(carried_docs, doc_ids, query_block, cycle_place, row_count)
        query_heads = carried.reshape(row_count, local_heads, POSITION_FREE + ROPE)
        carry_state = run_tile(carry_state, query_heads, key_rows, value_rows, rope_keys, visible)
    return_hops = WINDOW - 1
    sent = (carry_state[1], carry_state[2].reshape(row_count, local_heads * VDIM))
    returned = (
        passed_along(sent[0].astype(jnp.bfloat16), "ctx", return_hops).astype(jnp.float32),
        passed_along(sent[1].astype(jnp.bfloat16), "ctx", return_hops).astype(jnp.float32),
    )
    totals = jnp.repeat(returned[0], VDIM, axis=1)
    result = (returned[1] / totals).astype(jnp.bfloat16)
    return result


def solution(mesh):
    placed = (P("ctx", "dp"), P(("ctx", "dp"), None), P("ctx"), P(None, "dp"), P(None, "dp"))
    return jax.shard_map(
        on_device, mesh=mesh, in_specs=placed, out_specs=P("ctx", "dp"), check_vma=False
    )
```

profile of v0, /device:TPU:16, one launch (start us, length us, event | category | flops | bytes accessed | tf_op | source)
XLA Modules:
  0.0 346.9 jit_solution(2340115485758417990)
XLA Ops:
  0.0 5.3 %collective-permute-start.2 = (s32[512]{0:T(512)}, s32[512]{0:T(512)S(1)}, u32[]{:S(2)}, u32[]{:S(2)}) collective-permute-start(s32[512]{0:T(512)} %param.7), channel_id=1, source_target_pairs={{8,0},{16,8},{24,16},{32,24},{40,32},{48,40},{56,48},{64,56},{72,6... | collective-permute-start | bytes 6152 | tf_op jit(solution)/shard_map/ppermute | solution.py:21
  5.3 4.6 %copy.38 = bf16[512,3072]{0,1:T(8,128)(2,1)} copy(bf16[512,3072]{1,0:T(8,128)(2,1)} %param.5) | data formatting | bytes 6291456 | tf_op args[0]
  9.9 2.6 collective-permute-start.3
  12.6 67.1 %all_gather.3 = bf16[512,576]{1,0:T(8,128)(2,1)S(1)} all-gather(bf16[64,576]{1,0:T(8,128)(2,1)S(1)} %copy-done.5), channel_id=1, replica_groups=mesh['ctx'=16,'dp'=8] {'dp'}, dimensions={0}, use_global_device_ids=true | all-gather | bytes 663552 | tf_op jit(solution)/shard_map/all_gather | solution.py:93
  79.6 1.3 fusion.44
  80.9 0.5 copy-done.7
  81.5 2.6 convolution_convert_fusion
  84.1 0.8 copy-done.3
  84.9 8.1 %fusion.39 = f32[16,512,512]{2,1,0:T(8,128)} fusion(bf16[512,16,192]{0,2,1:T(8,128)(2,1)S(1)} %bitcast.73, bf16[64,16,8,128]{3,2,1,0:T(8,128)(2,1)S(1)} %fusion.44), kind=kOutput, calls=%fused_computation.42 | convolution fusion | flops 1073741824 | bytes 20971520 | tf_op jit(solution)/shard_map/thd,khd->thk/dot_general | solution.py:56
  93.0 0.0 collective-permute-done.2
  93.0 2.4 collective-permute-start.6
  95.4 2.9 copy.58
  98.3 1.0 and_and_fusion.1
  99.4 15.6 %fusion.63 = (f32[512,16]{0,1:T(8,128)S(1)}, f32[512,16,512]{0,2,1:T(8,128)}) fusion(bf16[512,16,192]{0,2,1:T(8,128)(2,1)} %bitcast.72, bf16[512,576]{1,0:T(8,128)(2,1)} %copy-done.4, f32[16,512,512]{2,1,0:T(8,128)} %fusion.39, pred[512,512]{0,1:T(8,128)(4,1)S(1)} %get-tuple-element.13), kind=kOutput, calls=%fused_computation.77 | convolution fusion | flops 553639936 | bytes 35028992 | tf_op jit(solution)/shard_map/thd,kd->thk/dot_general | solution.py:62
  115.0 0.6 broadcast_maximum_fusion
  115.6 8.6 %fusion.6 = f32[512,16]{0,1:T(8,128)S(1)} fusion(f32[512,16,512]{0,2,1:T(8,128)} %get-tuple-element.15, f32[512,16]{0,1:T(8,128)} %broadcast_maximum_fusion, pred[512,512]{0,1:T(8,128)(4,1)S(1)} %get-tuple-element.13), kind=kLoop, calls=%fused_computation.12 | loop fusion | flops 12574720 | bytes 17104896 | tf_op jit(solution)/shard_map/reduce_sum | solution.py:74
  124.2 0.6 exponential_multiply_fusion
  124.8 10.8 %bitcast_add_fusion.5 = f32[512,16,128]{0,2,1:T(8,128)} fusion(bf16[512,16,128]{0,2,1:T(8,128)(2,1)S(1)} %bitcast.68, f32[512,16,512]{0,2,1:T(8,128)} %get-tuple-element.15, f32[512,16]{0,1:T(8,128)} %broadcast_maximum_fusion, pred[512,512]{0,1:T(8,128)(4,1)S(1)} %get-tuple-element.13, f32[512,16]{0,1:T(8,128)S(1)} %get-tuple-element.9), kind=kOutput, calls=%fused_computation.35 | convolution fusion | flops 1087373312 | bytes 23396352 | tf_op jit(solution)/shard_map/thk,khd->thd/dot_general | solution.py:75
  135.7 3.1 collective-permute-start
  138.8 0.0 collective-permute-start.1
  138.9 0.2 collective-permute-start.9
  139.0 0.0 collective-permute-done.3
  139.0 4.6 %fusion.37 = f32[16,512,512]{2,1,0:T(8,128)S(1)} fusion(bf16[512,16,192]{0,2,1:T(8,128)(2,1)} %bitcast.6, bf16[64,16,8,128]{3,2,1,0:T(8,128)(2,1)} %copy-done.2), kind=kOutput, calls=%fused_computation.40 | convolution fusion | flops 1073741824 | bytes 20971520 | tf_op jit(solution)/shard_map/thd,khd->thk/dot_general | solution.py:56
  143.6 11.9 %fusion.64 = (f32[512,16]{0,1:T(8,128)}, f32[512,16,512]{0,2,1:T(8,128)}) fusion(bf16[512,16,192]{0,2,1:T(8,128)(2,1)} %bitcast.6, bf16[512,576]{1,0:T(8,128)(2,1)} %copy-done.4, f32[16,512,512]{2,1,0:T(8,128)S(1)} %fusion.37, pred[512,512]{0,1:T(8,128)(4,1)S(1)} %get-tuple-element.11), kind=kOutput, calls=%fused_computation.78 | convolution fusion | flops 553639936 | bytes 35028992 | tf_op jit(solution)/shard_map/thd,kd->thk/dot_general | solution.py:62
  155.5 1.9 collective-permute-start.7
  157.4 28.1 %collective-permute-done.1 = f32[512,16]{0,1:T(8,128)} collective-permute-done((f32[512,16]{0,1:T(8,128)}, f32[512,16]{0,1:T(8,128)}, u32[]{:S(2)}, u32[]{:S(2)}) %collective-permute-start.1) | collective-permute-done | bytes 32800 | tf_op jit(solution)/shard_map/ppermute | solution.py:27
  185.5 1.4 max.6
  186.9 8.6 %fusion.8 = f32[512,16]{0,1:T(8,128)S(1)} fusion(f32[512,16,512]{0,2,1:T(8,128)} %get-tuple-element.17, f32[512,16]{0,1:T(8,128)} %max.6, pred[512,512]{0,1:T(8,128)(4,1)S(1)} %get-tuple-element.11), kind=kLoop, calls=%fused_computation.14 | loop fusion | flops 12574720 | bytes 17104896 | tf_op jit(solution)/shard_map/reduce_sum | solution.py:74
  195.5 0.0 collective-permute-done.9
  195.5 1.4 multiply_add_fusion
  197.0 12.2 %bitcast_add_fusion.4 = f32[512,16,128]{0,2,1:T(8,128)} fusion(f32[512,16,128]{0,2,1:T(8,128)} %bitcast.5, bf16[512,16,128]{0,2,1:T(8,128)(2,1)S(1)} %bitcast.69, f32[512,16,512]{0,2,1:T(8,128)} %get-tuple-element.17, f32[512,16]{0,1:T(8,128)} %max.6, pred[512,512]{0,1:T(8,128)(4,1)S(1)} %get-tuple-element.11, f32[512,16]{0,1:T(8,128)S(1)} %get-tuple-element.8), kind=kOutput, calls=%fused_computation.34 | convolution fusion | flops 1088421888 | bytes 27590656 | tf_op jit(solution)/shard_map/thk,khd->thd/dot_general | solution.py:75
  209.2 5.8 %collective-permute-start.4 = (f32[512,2048]{0,1:T(8,128)}, f32[512,2048]{0,1:T(8,128)}, u32[]{:S(2)}, u32[]{:S(2)}) collective-permute-start(f32[512,2048]{0,1:T(8,128)} %bitcast.9), channel_id=1, source_target_pairs={{8,0},{16,8},{24,16},{32,24},{40,32},{48,40},{56,48},{64,56},{72,6... | collective-permute-start | bytes 12582920 | tf_op jit(solution)/shard_map/ppermute | solution.py:27
  215.0 0.1 collective-permute-start.5
  215.1 0.1 collective-permute-start.10
  215.1 4.4 %collective-permute-done.7 = bf16[512,3072]{0,1:T(8,128)(2,1)} collective-permute-done((bf16[512,3072]{0,1:T(8,128)(2,1)}, bf16[512,3072]{0,1:T(8,128)(2,1)}, u32[]{:S(2)}, u32[]{:S(2)}) %collective-permute-start.7) | collective-permute-done | bytes 3145760 | tf_op jit(solution)/shard_map/ppermute | solution.py:21
  219.6 4.5 %fusion.35 = f32[16,512,512]{2,1,0:T(8,128)S(1)} fusion(bf16[512,16,192]{0,2,1:T(8,128)(2,1)} %bitcast.11, bf16[64,16,8,128]{3,2,1,0:T(8,128)(2,1)} %copy-done.2), kind=kOutput, calls=%fused_computation.38 | convolution fusion | flops 1073741824 | bytes 20971520 | tf_op jit(solution)/shard_map/thd,khd->thk/dot_general | solution.py:56
  224.1 11.3 %fusion.65 = (f32[512,16]{0,1:T(8,128)S(1)}, f32[512,16,512]{0,2,1:T(8,128)}) fusion(bf16[512,16,192]{0,2,1:T(8,128)(2,1)} %bitcast.11, bf16[512,576]{1,0:T(8,128)(2,1)} %copy-done.4, f32[16,512,512]{2,1,0:T(8,128)S(1)} %fusion.35, pred[512,512]{0,1:T(8,128)(4,1)S(1)} %get-tuple-element.12), kind=kOutput, calls=%fused_computation.79 | convolution fusion | flops 553639936 | bytes 35028992 | tf_op jit(solution)/shard_map/thd,kd->thk/dot_general | solution.py:62
  235.4 29.4 %collective-permute-done.5 = f32[512,16]{0,1:T(8,128)S(1)} collective-permute-done((f32[512,16]{0,1:T(8,128)}, f32[512,16]{0,1:T(8,128)S(1)}, u32[]{:S(2)}, u32[]{:S(2)}) %collective-permute-start.5) | collective-permute-done | bytes 32800 | tf_op jit(solution)/shard_map/ppermute | solution.py:27
  264.9 8.6 %fusion.10 = f32[512,16]{0,1:T(8,128)S(1)} fusion(f32[512,16,512]{0,2,1:T(8,128)} %get-tuple-element.19, f32[512,16]{0,1:T(8,128)S(1)} %max.7, pred[512,512]{0,1:T(8,128)(4,1)S(1)} %get-tuple-element.12), kind=kLoop, calls=%fused_computation.16 | loop fusion | flops 12574720 | bytes 17104896 | tf_op jit(solution)/shard_map/reduce_sum | solution.py:74
  273.6 11.6 %fusion.28 = bf16[512,16,128]{0,2,1:T(8,128)(2,1)} fusion(f32[512,16,128]{0,2,1:T(8,128)} %bitcast.10, bf16[512,16,128]{0,2,1:T(8,128)(2,1)S(1)} %bitcast.70, f32[512,16,512]{0,2,1:T(8,128)} %get-tuple-element.19, f32[512,16]{0,1:T(8,128)S(1)} %max.7, pred[512,512]{0,1:T(8,128)(4,1)S(1)} %get-tuple-element.12, f32[512,16]{0,1:T(8,128)S(1)} %get-tuple-element.6), kind=kOutput, calls=%fused_computation.33 | convolution fusion | flops 1089470464 | bytes 25493504 | tf_op jit(solution)/shard_map/thk,khd->thd/dot_general | solution.py:75
  285.1 3.2 copy.53
  288.3 0.1 collective-permute-start.8
  288.4 0.1 collective-permute-start.11
  288.5 51.9 %collective-permute-done.11 = bf16[512,16]{0,1:T(8,128)(2,1)S(1)} collective-permute-done((bf16[512,16]{0,1:T(8,128)(2,1)S(1)}, bf16[512,16]{0,1:T(8,128)(2,1)S(1)}, u32[]{:S(2)}, u32[]{:S(2)}) %collective-permute-start.11) | collective-permute-done | bytes 16416 | tf_op jit(solution)/shard_map/ppermute | solution.py:27
  340.3 0.1 copy.54
  340.5 1.1 broadcast_in_dim.79
  341.6 0.0 copy-start.1
  341.6 5.0 %fusion.27 = bf16[512,2048]{1,0:T(8,128)(2,1)} fusion(f32[64,8,16,128]{3,2,1,0:T(8,128)S(1)} %bitcast.71, bf16[512,2048]{1,0:T(8,128)(2,1)} %collective-permute-done.8), kind=kLoop, calls=%fused_computation.31 | loop fusion | flops 3145728 | bytes 8388608 | tf_op jit(solution)/shard_map/convert_element_type | solution.py:125
  (23 shorter events, 0.1 us)
Async XLA Ops:
  0.0 79.6 %copy-start = (bf16[512,2048]{1,0:T(8,128)(2,1)S(1)}, bf16[512,2048]{1,0:T(8,128)(2,1)}, u32[]{:S(2)}) copy-start(bf16[512,2048]{1,0:T(8,128)(2,1)} %param.8) | copy-start | bytes 6291460
  0.0 12.6 %copy-start.5 = (bf16[64,576]{1,0:T(8,128)(2,1)S(1)}, bf16[64,576]{1,0:T(8,128)(2,1)}, u32[]{:S(2)}) copy-start(bf16[64,576]{1,0:T(8,128)(2,1)} %param.6) | copy-start | bytes 221188
  0.0 92.9 %collective-permute-start.2 = (s32[512]{0:T(512)}, s32[512]{0:T(512)S(1)}, u32[]{:S(2)}, u32[]{:S(2)}) collective-permute-start(s32[512]{0:T(512)} %param.7), channel_id=1, source_target_pairs={{8,0},{16,8},{24,16},{32,24},{40,32},{48,40},{56,48},{64,56},{72,6... | collective-permute-start | bytes 6152 | tf_op jit(solution)/shard_map/ppermute | solution.py:21
  9.9 129.1 %collective-permute-start.3 = (bf16[512,3072]{0,1:T(8,128)(2,1)}, bf16[512,3072]{0,1:T(8,128)(2,1)}, u32[]{:S(2)}, u32[]{:S(2)}) collective-permute-start(bf16[512,3072]{0,1:T(8,128)(2,1)} %copy.38), channel_id=1, source_target_pairs={{8,0},{16,8},{24,16},{32,24},{40,32},{48,40},{56,48},{64,56},{72,6... | collective-permute-start | bytes 9437192 | tf_op jit(solution)/shard_map/ppermute | solution.py:21
  79.6 1.3 copy-start.4
  79.6 1.8 copy-start.7
  81.5 2.6 copy-start.2
  81.5 3.4 copy-start.3
  92.9 5.4 %copy-start.6 = (s32[512]{0:T(512)S(1)}, s32[512]{0:T(512)}, u32[]{:S(2)}) copy-start(s32[512]{0:T(512)} %param.7) | copy-start | bytes 6148
  93.0 5.3 %collective-permute-start.6 = (s32[512]{0:T(512)S(1)}, s32[512]{0:T(512)S(1)}, u32[]{:S(2)}, u32[]{:S(2)}) collective-permute-start(s32[512]{0:T(512)S(1)} %collective-permute-done.2), channel_id=1, source_target_pairs={{8,0},{16,8},{24,16},{32,24},{40,32},{48,40},{56,48},{64,56},{72,6... | collective-permute-start | bytes 6152 | tf_op jit(solution)/shard_map/ppermute | solution.py:21
  135.7 61.3 %collective-permute-start = (f32[512,2048]{0,1:T(8,128)}, f32[512,2048]{0,1:T(8,128)}, u32[]{:S(2)}, u32[]{:S(2)}) collective-permute-start(f32[512,2048]{0,1:T(8,128)} %bitcast.4), channel_id=1, source_target_pairs={{8,0},{16,8},{24,16},{32,24},{40,32},{48,40},{56,48},{64,56},{72,6... | collective-permute-start | bytes 12582920 | tf_op jit(solution)/shard_map/ppermute | solution.py:27
  138.8 46.7 %collective-permute-start.1 = (f32[512,16]{0,1:T(8,128)}, f32[512,16]{0,1:T(8,128)}, u32[]{:S(2)}, u32[]{:S(2)}) collective-permute-start(f32[512,16]{0,1:T(8,128)} %broadcast_maximum_fusion), channel_id=1, source_target_pairs={{8,0},{16,8},{24,16},{32,24},{40,32},{48,40},{56,48},{64,56},{72,6... | collective-permute-start | bytes 98312 | tf_op jit(solution)/shard_map/ppermute | solution.py:27
  138.9 56.7 %collective-permute-start.9 = (f32[512,16]{0,1:T(8,128)}, f32[512,16]{0,1:T(8,128)}, u32[]{:S(2)}, u32[]{:S(2)}) collective-permute-start(f32[512,16]{0,1:T(8,128)} %get-tuple-element.10), channel_id=1, source_target_pairs={{8,0},{16,8},{24,16},{32,24},{40,32},{48,40},{56,48},{64,56},{72,6... | collective-permute-start | bytes 98312 | tf_op jit(solution)/shard_map/ppermute | solution.py:27
  155.5 64.0 %collective-permute-start.7 = (bf16[512,3072]{0,1:T(8,128)(2,1)}, bf16[512,3072]{0,1:T(8,128)(2,1)}, u32[]{:S(2)}, u32[]{:S(2)}) collective-permute-start(bf16[512,3072]{0,1:T(8,128)(2,1)} %collective-permute-done.3), channel_id=1, source_target_pairs={{8,0},{16,8},{24,16},{32,24},{40,32},{48,40},{56,48},{64,56},{72,6... | collective-permute-start | bytes 9437192 | tf_op jit(solution)/shard_map/ppermute | solution.py:21
  209.2 64.3 %collective-permute-start.4 = (f32[512,2048]{0,1:T(8,128)}, f32[512,2048]{0,1:T(8,128)}, u32[]{:S(2)}, u32[]{:S(2)}) collective-permute-start(f32[512,2048]{0,1:T(8,128)} %bitcast.9), channel_id=1, source_target_pairs={{8,0},{16,8},{24,16},{32,24},{40,32},{48,40},{56,48},{64,56},{72,6... | collective-permute-start | bytes 12582920 | tf_op jit(solution)/shard_map/ppermute | solution.py:27
  215.0 49.9 %collective-permute-start.5 = (f32[512,16]{0,1:T(8,128)}, f32[512,16]{0,1:T(8,128)S(1)}, u32[]{:S(2)}, u32[]{:S(2)}) collective-permute-start(f32[512,16]{0,1:T(8,128)} %max.6), channel_id=1, source_target_pairs={{8,0},{16,8},{24,16},{32,24},{40,32},{48,40},{56,48},{64,56},{72,6... | collective-permute-start | bytes 98312 | tf_op jit(solution)/shard_map/ppermute | solution.py:27
  215.1 58.5 %collective-permute-start.10 = (f32[512,16]{0,1:T(8,128)}, f32[512,16]{0,1:T(8,128)S(1)}, u32[]{:S(2)}, u32[]{:S(2)}) collective-permute-start(f32[512,16]{0,1:T(8,128)} %get-tuple-element.7), channel_id=1, source_target_pairs={{8,0},{16,8},{24,16},{32,24},{40,32},{48,40},{56,48},{64,56},{72,6... | collective-permute-start | bytes 98312 | tf_op jit(solution)/shard_map/ppermute | solution.py:27
  288.3 52.1 %collective-permute-start.8 = (bf16[512,2048]{1,0:T(8,128)(2,1)S(1)}, bf16[512,2048]{1,0:T(8,128)(2,1)}, u32[]{:S(2)}, u32[]{:S(2)}) collective-permute-start(bf16[512,2048]{1,0:T(8,128)(2,1)S(1)} %copy.53), channel_id=1, source_target_pairs={{112,0},{120,8},{0,16},{8,24},{16,32},{24,40},{32,48},{40,56},{48,... | collective-permute-start | bytes 6291464 | tf_op jit(solution)/shard_map/ppermute | solution.py:27
  288.4 51.9 %collective-permute-start.11 = (bf16[512,16]{0,1:T(8,128)(2,1)S(1)}, bf16[512,16]{0,1:T(8,128)(2,1)S(1)}, u32[]{:S(2)}, u32[]{:S(2)}) collective-permute-start(bf16[512,16]{0,1:T(8,128)(2,1)S(1)} %get-tuple-element.5), channel_id=1, source_target_pairs={{112,0},{120,8},{0,16},{8,24},{16,32},{24,40},{32,48},{40,56},{48,... | collective-permute-start | bytes 49160 | tf_op jit(solution)/shard_map/ppermute | solution.py:27
  341.6 5.1 %copy-start.1 = (bf16[512,2048]{1,0:T(8,128)(2,1)S(1)}, bf16[512,2048]{1,0:T(8,128)(2,1)}, u32[]{:S(2)}) copy-start(bf16[512,2048]{1,0:T(8,128)(2,1)} %param.8) | copy-start | bytes 6291460
where the time goes:
time: 352 us; the launch traced here: 347 us
  waiting for transfers between devices  114 us (32%)
  matrix products  94.6 us (27%)
  blocking collectives  67.1 us (19%)
  other arithmetic  36 us (10%)
  starting transfers between devices  21.6 us (6%)
  local copies, waits for them, and re-layouts  13.3 us (4%)
    ppermute x8, waiting for transfers between devices, passed_along(): return lax.ppermute(block, axis, route)  109 us
    all_gather x1, blocking collectives, on_device(): latent_block = lax.all_gather(latent_cache, 'dp', axis=0, tiled=True)  67.1 us
    dot_general x3, matrix products, attend(): jnp.einsum('thd,kd->thk', query_heads[..., POSITION_FREE:], rope_keys, pr...  38.9 us
    dot_general x3, matrix products, attend(): jnp.einsum('thk,khd->thd', softmax_weights.astype(jnp.bfloat16), value_ro...  34.7 us
    reduce_sum x3, other arithmetic, attend(): weight_sum = weight_sum * factor + jnp.sum(softmax_weights, axis=2)  25.9 us
    dot_general x3, matrix products, attend(): jnp.einsum('thd,khd->thk', query_heads[..., :POSITION_FREE], key_rows, pr...  17.2 us
    ppermute x4, starting transfers between devices, shifted(): lax.ppermute(value, axis, [(source, source + steps) for source in range(i...  12.2 us
    ppermute x8, starting transfers between devices, passed_along(): return lax.ppermute(block, axis, route)  9.4 us
  transfers between devices with their start and end apart: 12, of which 4 were waited for; matrix products, arithmetic and copies ran while one was open for 35% of the time, Pallas kernels for 0%

commit v1 on v0

v1 whole, which is shorter than its diff:
```python
import functools
import math

import jax
import jax.numpy as jnp
from jax import lax
from jax.experimental import pallas as pl
from jax.experimental.pallas import tpu as pltpu
from jax.sharding import PartitionSpec as P

MESH = pl.DeviceIdType.MESH
SHARDS = 8


def gather_kernel(lat_ref, docs_ref, lat_out, docs_out, lat_s, docs_s, send, recv, relay_send, relay_recv, misc_send, misc_recv, out_sem):
    ctx, dp = lax.axis_index("ctx"), lax.axis_index("dp")
    x, y, core = dp // 2, dp % 2, ctx % 2
    right_x, left_x, far_x = (x + 1) % 4, (x + 3) % 4, (x + 2) % 4
    partner = (ctx, x * 2 + 1 - y)
    right, left = (ctx, right_x * 2 + y), (ctx, left_x * 2 + y)
    next1, next2 = ((ctx + 1) % 16, dp), ((ctx + 2) % 16, dp)
    prev1, prev2 = ((ctx + 15) % 16, dp), ((ctx + 14) % 16, dp)
    sibling = (ctx + 1 - 2 * core, dp)
    shard = [column * 2 + row for column in (x, left_x, right_x, far_x) for row in (y, 1 - y)]

    barrier = pltpu.get_barrier_semaphore()
    for peer in (partner, right, left, next1, next2, prev1, prev2):
        pl.semaphore_signal(barrier, inc=1, device_id=peer, device_id_type=MESH)
    pl.semaphore_wait(barrier, 7)

    def remote(src, dst, send_sem, recv_sem, peer):
        return pltpu.make_async_remote_copy(
            src_ref=src, dst_ref=dst, send_sem=send_sem, recv_sem=recv_sem, device_id=peer, device_id_type=MESH)

    def piece(w, k, half=None):
        block = lat_s.at[2 * w, shard[k]]
        return block if half is None else block.at[pl.ds(32 * half, 32)]

    def copy(w, slot, src, dst, peer):
        return remote(src, dst, send.at[w, slot], recv.at[w, slot], peer)

    def to_partner(w, src):
        return copy(w, 0, src, piece(w, 0), partner)

    def to_right(w, k, src):
        return copy(w, 1 + k, src, piece(w, k), right)

    def to_left(w, k, src):
        return copy(w, 3 + k, src, piece(w, k), left)

    def on_right(w, k):
        return copy(w, 5 + k, piece(w, 2 + k, 0), piece(w, 2 + k, 0), right)

    def on_left(w, k):
        return copy(w, 7 + k, piece(w, 4 + k, 1), piece(w, 4 + k, 1), left)

    def got(w, slot):
        k, half = [(1, None), (2, None), (3, None), (4, None), (5, None), (6, 0), (7, 0), (6, 1), (7, 1)][slot]
        place = piece(w, k, half)
        copy(w, slot, place, place, partner).wait_recv()

    def relay(k):
        src = lat_s.at[2 - 2 * core, shard[k]]
        return remote(src, lat_s.at[1, shard[k]], relay_send.at[k], relay_recv.at[k], sibling)

    def relay_if(w, k):
        @pl.when(core == 1 - w)
        def _():
            relay(k).start()

    zc = remote(lat_ref, lat_s.at[0, dp], misc_send.at[0], misc_recv.at[0], next2)
    d1 = remote(docs_ref, docs_s.at[1], misc_send.at[1], misc_recv.at[1], next1)
    d2 = remote(docs_ref, docs_s.at[0], misc_send.at[2], misc_recv.at[2], next2)
    mine = pltpu.make_async_copy(lat_ref, lat_s.at[2, dp], misc_send.at[3])
    docs_mine = pltpu.make_async_copy(docs_ref, docs_s.at[2], misc_send.at[4])
    started = []

    def go(c):
        c.start()
        started.append(c)

    go(zc)
    mine.start()
    docs_mine.start()
    go(to_partner(1, lat_ref))
    go(to_right(1, 0, lat_ref))
    go(to_left(1, 0, lat_ref))
    go(d1)
    go(d2)
    mine.wait()
    relay_if(1, 0)
    zc.wait_recv()
    go(to_partner(0, piece(0, 0)))
    go(to_right(0, 0, piece(0, 0)))
    go(to_left(0, 0, piece(0, 0)))
    relay_if(0, 0)
    for w in (1, 0):
        got(w, 0)
        go(to_right(w, 1, piece(w, 1)))
        go(to_left(w, 1, piece(w, 1)))
        relay_if(w, 1)
    for w in (1, 0):
        for k in range(2):
            got(w, 1 + k)
            go(on_right(w, k))
            relay_if(w, 2 + k)
            got(w, 3 + k)
            go(on_left(w, k))
            relay_if(w, 4 + k)
    for w in (1, 0):
        for k in range(2):
            got(w, 5 + k)
            got(w, 7 + k)
            relay_if(w, 6 + k)
    outs = [pltpu.make_async_copy(lat_s.at[2 * w], lat_out.at[2 * w], out_sem.at[w]) for w in range(2)]
    for o in outs:
        o.start()
    for k in range(8):
        place = lat_s.at[1, shard[k]]
        remote(place, place, relay_send.at[k], relay_recv.at[k], sibling).wait_recv()
    last = pltpu.make_async_copy(lat_s.at[1], lat_out.at[1], out_sem.at[2])
    last.start()
    docs_mine.wait()
    d1.wait_recv()
    d2.wait_recv()
    docs_out[...] = docs_s[...]
    for o in outs:
        o.wait()
    last.wait()
    for c in started:
        c.wait_send()
    for k in range(8):
        relay(k).wait_send()


def gather(latent, docs):
    return pl.pallas_call(
        gather_kernel,
        out_shape=(jax.ShapeDtypeStruct((3, SHARDS, 64, 576), jnp.bfloat16), jax.ShapeDtypeStruct((3, 4, 128), jnp.int32)),
        in_specs=[pl.BlockSpec(memory_space=pltpu.VMEM)] * 2,
        out_specs=(pl.BlockSpec(memory_space=pl.ANY), pl.BlockSpec(memory_space=pltpu.VMEM)),
        scratch_shapes=[
            pltpu.VMEM((3, SHARDS, 64, 576), jnp.bfloat16),
            pltpu.VMEM((3, 4, 128), jnp.int32),
            pltpu.SemaphoreType.DMA((2, 9)),
            pltpu.SemaphoreType.DMA((2, 9)),
            pltpu.SemaphoreType.DMA((8,)),
            pltpu.SemaphoreType.DMA((8,)),
            pltpu.SemaphoreType.DMA((5,)),
            pltpu.SemaphoreType.DMA((3,)),
            pltpu.SemaphoreType.DMA((3,)),
        ],
        compiler_params=pltpu.CompilerParams(collective_id=0, has_side_effects=True, vmem_limit_bytes=20 * 2**20),
    )(latent, docs)


BIG = 1e30
C = math.log2(math.e) / math.sqrt(192)
LOW, HIGH = 2.0 ** -60, 2.0 ** 100
T = 256
NT = (((1,), (1,)), ((), ()))

def build_tails(docs_ref, lat_ref, tail_ref, qtail_ref):
    lane = lax.broadcasted_iota(jnp.int32, (128, 128), 1)
    for g in range(12):
        b, r = divmod(g, 4)
        row = jnp.broadcast_to(docs_ref[b, r:r + 1, :], (128, 128))
        col = jnp.transpose(row.astype(jnp.float32)).astype(jnp.int32)
        rope = lat_ref[g * 128:(g + 1) * 128, 512:576].astype(jnp.float32)
        rope = jnp.concatenate([rope, jnp.zeros((128, 64), jnp.float32)], axis=1)
        other = (lane >= 64) & (lane < 80) & (col != lane - 64)
        tail_ref[g * 128:(g + 1) * 128, :] = jnp.where(other, -BIG, rope).astype(jnp.bfloat16)
        if b == 2:
            qtail_ref[r * 128:(r + 1) * 128, :] = (col == lane - 64).astype(jnp.float32).astype(jnp.bfloat16)

def kernel(HP, q_ref, docs_ref, lat_ref, wk_ref, wv_ref, o_ref, k_s, v_s, q_s, tail_s, qtail_s, rng_s):
    @pl.when(pl.program_id(0) == 0)
    def _():
        build_tails(docs_ref, lat_ref, tail_s, qtail_s)

    def doc_at(i):
        b, r = divmod(i, 512)
        r, l = divmod(r, 128)
        return docs_ref[b, r, l]

    firsts = []
    for qb in range(2):
        head_doc = doc_at(1024 + qb * T)
        lo = jnp.int32(4 + qb)
        for c in reversed(range(qb, 4 + qb)):
            lo = jnp.where(doc_at(c * T + T - 1) == head_doc, c, lo)
        firsts.append(lo)
    first = jnp.minimum(firsts[0], firsts[1])
    for c in range(6):
        @pl.when((c >= first))
        def _(c=c):
            rows = pl.ds(c * T, T)
            lat = lat_ref[rows, :512]
            k_s[rows, :] = (jnp.dot(lat, wk_ref[...], preferred_element_type=jnp.float32)).astype(jnp.bfloat16)
            v_s[rows, :] = jnp.dot(lat, wv_ref[...], preferred_element_type=jnp.float32).astype(jnp.bfloat16)

    half = lax.broadcasted_iota(jnp.int32, (512, 128), 1) < 64
    qtail = qtail_s[...]
    for p in range(HP // 2):
        o = p * 384
        q_s[2 * p, :, :128] = q_ref[:, o:o + 128]
        q_s[2 * p, :, 128:] = jnp.where(half, q_ref[:, o + 128:o + 256], qtail)
        q_s[2 * p + 1, :, :128] = q_ref[:, o + 192:o + 320]
        rope = jnp.concatenate([q_ref[:, o + 320:o + 384], qtail[:, 64:]], axis=1)
        q_s[2 * p + 1, :, 128:] = rope

    ones = jnp.ones((T, 128), jnp.bfloat16)
    causal = lax.broadcasted_iota(jnp.int32, (T, T), 1) <= lax.broadcasted_iota(jnp.int32, (T, T), 0)

    def score(h, qb, c, diag):
        rows = pl.ds(c * T, T)
        keys = jnp.concatenate([k_s[rows, h * 128:(h + 1) * 128], tail_s[rows, :]], axis=1)
        s = lax.dot_general(q_s[h, pl.ds(qb * T, T), :], keys, NT, preferred_element_type=jnp.float32)
        s = s * C
        return jnp.where(causal, s, -BIG) if diag else s

    def values(h, c):
        return jnp.concatenate([v_s[pl.ds(c * T, T), h * 128:(h + 1) * 128], ones], axis=1)

    for qb in range(2):
        for n in range(1, 6):
            @pl.when((firsts[qb] == 5 + qb - n))
            def _(qb=qb, n=n):
                for h in range(HP):
                    end = 4 + qb
                    acc = None
                    for c in range(end - n + 1, end + 1):
                        p = jnp.exp2(score(h, qb, c, c == end)).astype(jnp.bfloat16)
                        t = jnp.dot(p, values(h, c), preferred_element_type=jnp.float32)
                        acc = t if acc is None else acc + t
                    total = acc[:, 128:]
                    o_ref[qb * T:(qb + 1) * T, h * 128:(h + 1) * 128] = (acc[:, :128] / total).astype(jnp.bfloat16)
                    if h == 0 and qb == 0:
                        rng_s[0], rng_s[1] = total, total
                    else:
                        rng_s[0] = jnp.minimum(rng_s[0], total)
                        rng_s[1] = jnp.maximum(rng_s[1], total)

    inside = (jnp.min(rng_s[0]) >= LOW) & (jnp.max(rng_s[1]) <= HIGH)

    @pl.when(jnp.logical_not(inside))
    def _():
        for qb in range(2):
            end = 4 + qb
            for h in range(HP):
                def body(c, state):
                    peak, acc = state
                    s = score(h, qb, c, False)
                    s = jnp.where(causal | (c < end), s, -BIG)
                    new = jnp.maximum(peak, jnp.max(s, axis=1, keepdims=True))
                    p = jnp.exp2(s - new).astype(jnp.bfloat16)
                    acc = acc * jnp.exp2(peak - new) + jnp.dot(p, values(h, c), preferred_element_type=jnp.float32)
                    return new, acc
                _, acc = lax.fori_loop(firsts[qb], end + 1, body, (jnp.full((T, 1), -BIG, jnp.float32), jnp.zeros((T, 256), jnp.float32)))
                o_ref[qb * T:(qb + 1) * T, h * 128:(h + 1) * 128] = (acc[:, :128] / acc[:, 128:]).astype(jnp.bfloat16)

def attend(q, docs, lat, wk, wv, HP=2):
    H = wk.shape[1] // 128
    return pl.pallas_call(
        functools.partial(kernel, HP),
        out_shape=jax.ShapeDtypeStruct((512, H * 128), jnp.bfloat16),
        grid_spec=pltpu.PrefetchScalarGridSpec(
            num_scalar_prefetch=0,
            grid=(H // HP,),
            in_specs=[
                pl.BlockSpec((512, HP * 192), lambda i: (0, i)),
                pl.BlockSpec((3, 4, 128), lambda i: (0, 0, 0)),
                pl.BlockSpec((1536, 576), lambda i: (0, 0)),
                pl.BlockSpec((512, HP * 128), lambda i: (0, i)),
                pl.BlockSpec((512, HP * 128), lambda i: (0, i)),
            ],
            out_specs=pl.BlockSpec((512, HP * 128), lambda i: (0, i)),
            scratch_shapes=[
                pltpu.VMEM((1536, HP * 128), jnp.bfloat16),
                pltpu.VMEM((1536, HP * 128), jnp.bfloat16),
                pltpu.VMEM((HP, 512, 256), jnp.bfloat16),
                pltpu.VMEM((1536, 128), jnp.bfloat16),
                pltpu.VMEM((512, 128), jnp.bfloat16),
                pltpu.VMEM((2, T, 128), jnp.float32),
            ]),
        compiler_params=pltpu.CompilerParams(vmem_limit_bytes=50 * 2**20),
    )(q, docs, lat, wk, wv)


def on_device(queries, latent_cache, doc_ids, w_key, w_value):
    window, docs = gather(latent_cache, doc_ids.reshape(4, 128))
    return attend(queries, docs, window.reshape(1536, 576), w_key, w_value, 8)


def solution(mesh):
    placed = (P("ctx", "dp"), P(("ctx", "dp"), None), P("ctx"), P(None, "dp"), P(None, "dp"))
    return jax.shard_map(on_device, mesh=mesh, in_specs=placed, out_specs=P("ctx", "dp"), check_vma=False)
```

time: 352 us -> 119 us (0.34); the launches traced: 347 us -> 119 us
  Pallas kernels: 0 us -> 116 us
  waiting for transfers between devices: 114 us -> 0 us
  matrix products: 94.6 us -> 0 us
  blocking collectives: 67.1 us -> 0 us
  other arithmetic: 36 us -> 0 us
  starting transfers between devices: 21.6 us -> 0 us
  local copies, waits for them, and re-layouts: 13.3 us -> 3.15 us
    pallas_call x0 -> x2, Pallas kernels: none -> 116 us  [the longest x1 92.9 us: attend(): pl.pallas_call(functools.partial(kernel, HP), out_shape=jax.ShapeDtypeStr...]
    ppermute x12 -> x0, waiting for transfers between devices: 114 us -> none  [the longest x8 109 us: passed_along(): return lax.ppermute(block, axis, route)]
    dot_general x11 -> x0, matrix products: 94.6 us -> none  [the longest x3 38.9 us: attend(): jnp.einsum('thd,kd->thk', query_heads[..., POSITION_FREE:], rope_keys, pr...]
    all_gather x1 -> x0, blocking collectives: 67.1 us -> none  [on_device(): latent_block = lax.all_gather(latent_cache, 'dp', axis=0, tiled=True)]
    reduce_sum x3 -> x0, other arithmetic: 25.9 us -> none  [attend(): weight_sum = weight_sum * factor + jnp.sum(softmax_weights, axis=2)]
    ppermute x12 -> x0, starting transfers between devices: 21.6 us -> none  [the longest x4 12.2 us: shifted(): lax.ppermute(value, axis, [(source, source + steps) for source in range(i...]
    convert_element_type x2 -> x0, other arithmetic: 5.06 us -> none  [the longest x1 5.04 us: on_device(): result = (returned[1] / totals).astype(jnp.bfloat16)]
  transfers between devices with their start and end apart: 12 -> 0, of which waited for: 4 -> 0; matrix products, arithmetic and copies ran while one was open for 35% -> 0% of each run, Pallas kernels for 0% -> 0%
where the time goes in v1:
time: 119 us
  Pallas kernels  116 us (97%)
  local copies, waits for them, and re-layouts  3.15 us (3%)
    pallas_call x1, Pallas kernels, attend(): pl.pallas_call(functools.partial(kernel, HP), out_shape=jax.ShapeDtypeStr...  92.9 us
    pallas_call x1, Pallas kernels, gather(): pl.pallas_call(gather_kernel, out_shape=(jax.ShapeDtypeStruct((3, SHARDS,...  22.7 us
    unnamed x6, local copies, waits for them, and re-layouts  3.15 us

profile of v1, /device:TPU:16, one launch (start us, length us, event | category | flops | bytes accessed | tf_op | source)
XLA Modules:
  0.0 118.7 jit_solution(2161367745650560917)
XLA Ops:
  0.0 0.0 copy-start.1
  0.0 0.9 copy-done.1
  0.9 0.0 copy-start.2
  0.9 0.7 copy-done.2
  1.6 22.7 %shard_map.55 = (bf16[3,8,64,576]{3,2,1,0:T(8,128)(2,1)S(1)}, s32[3,4,128]{2,1,0:T(4,128)S(1)}) custom-call(bf16[64,576]{1,0:T(8,128)(2,1)S(1)} %copy-done.1, s32[4,128]{1,0:T(4,128)S(1)} %bitcast.3), custom_call_target="tpu_custom_call" | custom-call | tf_op jit(solution)/shard_map/pallas_call | solution.py:137
  24.3 0.0 copy-start
  24.3 1.6 %copy-done = bf16[512,2048]{1,0:T(8,128)(2,1)S(1)} copy-done((bf16[512,2048]{1,0:T(8,128)(2,1)S(1)}, bf16[512,2048]{1,0:T(8,128)(2,1)}, u32[]{:S(2)}) %copy-start) | copy-done | bytes 2097176
  25.9 92.9 %shard_map.56 = bf16[512,2048]{1,0:T(8,128)(2,1)} custom-call(bf16[512,3072]{1,0:T(8,128)(2,1)} %q_ref.1, s32[3,4,128]{2,1,0:T(4,128)S(1)} %get-tuple-element.7.docs_ref, bf16[1536,576]{1,0:T(8,128)(2,1)S(1)} %bitcast.2, bf16[512,2048]{1,0:T(8,128)(2,1)S(1)} %copy-done, bf16[512,2048]{1,0:T(8,128)(2,1)} %wv_ref.1), custom_call_target="tpu_custom_call" | custom-call | tf_op jit(solution)/shard_map/pallas_call | solution.py:264
Async XLA Ops:
  0.0 0.9 copy-start.1
  0.9 0.7 copy-start.2
  24.3 1.6 %copy-start = (bf16[512,2048]{1,0:T(8,128)(2,1)S(1)}, bf16[512,2048]{1,0:T(8,128)(2,1)}, u32[]{:S(2)}) copy-start(bf16[512,2048]{1,0:T(8,128)(2,1)} %wk_ref.1) | copy-start | bytes 6291460

commit v2 on v0

v2 whole, which is shorter than its diff:
```python
import functools
import math

import jax
import jax.numpy as jnp
from jax import lax
from jax.experimental import pallas as pl
from jax.experimental.pallas import tpu as pltpu
from jax.sharding import PartitionSpec as P

MESH = pl.DeviceIdType.MESH
BF16, F32 = jnp.bfloat16, jnp.float32
HEADS = 16
GROUP = 4
T = 256
BIG = 1e30
SCALE = math.log2(math.e) / math.sqrt(192)
LOW, HIGH = 2.0 ** -60, 2.0 ** 100
NT = (((1,), (1,)), ((), ()))


def scores(query, keys):
    return lax.dot_general(query, keys, NT, preferred_element_type=F32) * SCALE


def with_ones(value):
    return jnp.concatenate([value, jnp.ones((value.shape[0], 128), BF16)], axis=1)


def expand(rows, weight):
    return jnp.dot(rows, weight, preferred_element_type=F32).astype(BF16)


def documents_down(row):
    return jnp.transpose(jnp.broadcast_to(row, (128, 128)).astype(F32)).astype(jnp.int32)


def key_tail(rope, row):
    lane = lax.broadcasted_iota(jnp.int32, (128, 128), 1)
    other = (lane >= 64) & (lane < 80) & (documents_down(row) != lane - 64)
    rope = jnp.concatenate([rope.astype(F32), jnp.zeros((128, 64), F32)], axis=1)
    return jnp.where(other, -BIG, rope).astype(BF16)


def query_tail(row):
    lane = lax.broadcasted_iota(jnp.int32, (128, 128), 1)
    return (documents_down(row) == lane - 64).astype(F32).astype(BF16)


def causal_mask():
    return lax.broadcasted_iota(jnp.int32, (T, T), 1) <= lax.broadcasted_iota(jnp.int32, (T, T), 0)


def gather_kernel(lat_ref, docs_ref, q_ref, wk_ref, wv_ref,
                  lat_s, docs_s, qp, wk_s, wv_s, acc_s,
                  q_s, k_s, v_s, tail_s, qtail_s,
                  send, recv, relay_send, relay_recv, misc_send, misc_recv, load_sem):
    ctx, dp = lax.axis_index("ctx"), lax.axis_index("dp")
    x, y, core = dp // 2, dp % 2, ctx % 2
    right_x, left_x, far_x = (x + 1) % 4, (x + 3) % 4, (x + 2) % 4
    partner = (ctx, x * 2 + 1 - y)
    right, left = (ctx, right_x * 2 + y), (ctx, left_x * 2 + y)
    next1, next2 = ((ctx + 1) % 16, dp), ((ctx + 2) % 16, dp)
    prev1, prev2 = ((ctx + 15) % 16, dp), ((ctx + 14) % 16, dp)
    sibling = (ctx + 1 - 2 * core, dp)
    shard = [column * 2 + row for column in (x, left_x, right_x, far_x) for row in (y, 1 - y)]

    barrier = pltpu.get_barrier_semaphore()
    for peer in (partner, right, left, next1, next2, prev1, prev2):
        pl.semaphore_signal(barrier, inc=1, device_id=peer, device_id_type=MESH)

    loads = [pltpu.make_async_copy(src, dst, load_sem.at[i]) for i, (src, dst) in enumerate((
        (lat_ref, lat_s.at[2, dp]), (docs_ref, docs_s.at[2]), (q_ref, q_s), (wk_ref, wk_s), (wv_ref, wv_s)))]
    for c in loads:
        c.start()
    pl.semaphore_wait(barrier, 7)

    def remote(src, dst, send_sem, recv_sem, peer):
        return pltpu.make_async_remote_copy(
            src_ref=src, dst_ref=dst, send_sem=send_sem, recv_sem=recv_sem, device_id=peer, device_id_type=MESH)

    def piece(w, k, half=None):
        block = lat_s.at[2 * w, shard[k]]
        return block if half is None else block.at[pl.ds(32 * half, 32)]

    brings = {
        1: [(1, None), (2, None), (3, None), (4, None), (5, None), (6, 0), (7, 0), (6, 1), (7, 1)],
        0: [(1, None), (2, None), (4, None), (6, 0), (6, 1), (3, None), (5, None), (7, None)],
    }
    started = []

    def go(w, slot, src, dst, peer):
        c = remote(src, dst, send.at[w, slot], recv.at[w, slot], peer)
        c.start()
        started.append(c)

    def got(w, slot):
        place = piece(w, *brings[w][slot])
        remote(place, place, send.at[w, slot], recv.at[w, slot], partner).wait_recv()

    def same(w, slot, k, peer, half=None):
        go(w, slot, piece(w, k, half), piece(w, k, half), peer)

    def relay(k):
        return remote(lat_s.at[2 - 2 * core, shard[k]], lat_s.at[1, shard[k]], relay_send.at[k], relay_recv.at[k], sibling)

    def relay_if(w, k):
        @pl.when(core == 1 - w)
        def _():
            relay(k).start()

    onward = remote(lat_ref, lat_s.at[0, dp], misc_send.at[0], misc_recv.at[0], next2)
    stay = pltpu.make_async_copy(lat_ref, lat_s.at[0, dp], misc_recv.at[3])
    d1 = remote(docs_ref, docs_s.at[1], misc_send.at[1], misc_recv.at[1], next1)
    d2 = remote(docs_ref, docs_s.at[0], misc_send.at[2], misc_recv.at[2], next2)

    go(1, 0, lat_ref, piece(1, 0), partner)
    go(1, 1, lat_ref, piece(1, 0), right)
    go(1, 3, lat_ref, piece(1, 0), left)

    @pl.when(ctx < 14)
    def _():
        onward.start()

    @pl.when(ctx < 2)
    def _():
        stay.start()

    d1.start()
    d2.start()
    loads[0].wait()
    relay_if(1, 0)

    got(1, 0)
    same(1, 2, 1, right)
    same(1, 4, 1, left)
    relay_if(1, 1)

    @pl.when(ctx >= 2)
    def _():
        onward.wait_recv()

    @pl.when(ctx < 2)
    def _():
        stay.wait()

    same(0, 1, 0, right)
    same(0, 2, 0, left)
    same(0, 0, 0, partner)
    relay_if(0, 0)

    loads[1].wait()
    for r in range(4):
        qtail_s[pl.ds(128 * r, 128), :] = query_tail(docs_s[2, r:r + 1, :])
    loads[2].wait()
    qtail = qtail_s[...]

    def prepare(p, carry):
        a, b, c = [q_s[:, pl.ds(pl.multiple_of(p * 384 + 128 * i, 128), 128)] for i in range(3)]
        qp[2 * p, :, :128] = a
        qp[2 * p, :, 128:] = jnp.concatenate([b[:, :64], qtail[:, 64:]], axis=1)
        qp[2 * p + 1, :, :128] = jnp.concatenate([b[:, 64:], c[:, :64]], axis=1)
        qp[2 * p + 1, :, 128:] = jnp.concatenate([c[:, 64:], qtail[:, 64:]], axis=1)
        return carry

    lax.fori_loop(0, HEADS // 2, prepare, 0)

    got(1, 1)
    same(1, 5, 2, right, 0)
    relay_if(1, 2)
    got(1, 3)
    same(1, 7, 4, left, 1)
    relay_if(1, 4)
    got(1, 2)
    same(1, 6, 3, right, 0)
    relay_if(1, 3)
    got(1, 4)
    same(1, 8, 5, left, 1)
    relay_if(1, 5)
    got(0, 1)
    same(0, 3, 2, right, 0)
    same(0, 5, 2, partner)
    relay_if(0, 2)
    got(0, 2)
    same(0, 4, 4, left, 1)
    same(0, 6, 4, partner)
    relay_if(0, 4)
    got(1, 5)
    got(1, 7)
    relay_if(1, 6)
    got(1, 6)
    got(1, 8)
    relay_if(1, 7)

    loads[3].wait()
    loads[4].wait()
    for r in range(4):
        rope = lat_s[2, 2 * r:2 * r + 2, :, 512:].reshape(128, 64)
        tail_s[pl.ds(128 * r, 128), :] = key_tail(rope, docs_s[2, r:r + 1, :])

    def own(g, carry):
        columns = pl.ds(pl.multiple_of(g * GROUP * 128, 128), GROUP * 128)
        latent = lat_s[2, :, :, :512].reshape(512, 512)
        k_s[...] = expand(latent, wk_s[:, columns])
        v_s[...] = expand(latent, wv_s[:, columns])
        causal = causal_mask()
        tail = tail_s[...]
        for h in range(GROUP):
            head = g * GROUP + h
            keys = jnp.concatenate([k_s[:, h * 128:(h + 1) * 128], tail], axis=1)
            value = with_ones(v_s[:, h * 128:(h + 1) * 128])
            for qb in range(2):
                s = scores(qp[head, pl.ds(qb * T, T), :], keys[:(qb + 1) * T])
                diagonal = jnp.where(causal, s[:, qb * T:], -BIG)
                s = diagonal if qb == 0 else jnp.concatenate([s[:, :T], diagonal], axis=1)
                weights = jnp.exp2(s).astype(BF16)
                acc_s[head, pl.ds(qb * T, T), :] = jnp.dot(weights, value[:(qb + 1) * T], preferred_element_type=F32)
        return carry

    lax.fori_loop(0, 1, own, 0)
    got(0, 3)
    got(0, 4)
    same(0, 7, 6, partner)
    relay_if(0, 6)
    got(0, 0)
    relay_if(0, 1)
    got(0, 5)
    relay_if(0, 3)
    got(0, 6)
    relay_if(0, 5)
    lax.fori_loop(1, 2, own, 0)
    got(0, 7)
    relay_if(0, 7)
    lax.fori_loop(2, HEADS // GROUP, own, 0)

    d1.wait_recv()
    d2.wait_recv()
    for k in range(8):
        place = lat_s.at[1, shard[k]]
        remote(place, place, relay_send.at[k], relay_recv.at[k], sibling).wait_recv()
    for c in started:
        c.wait_send()
    for k in range(8):
        relay(k).wait_send()
    d1.wait_send()
    d2.wait_send()

    @pl.when(ctx < 14)
    def _():
        onward.wait_send()


def gather(latent, docs, queries, w_key, w_value):
    vmem, hbm = pl.BlockSpec(memory_space=pltpu.VMEM), pl.BlockSpec(memory_space=pltpu.HBM)
    operands = [pltpu.with_memory_space_constraint(a, pltpu.HBM) for a in (latent, docs, queries, w_key, w_value)]
    return pl.pallas_call(
        gather_kernel,
        out_shape=(
            pltpu.VMEM((3, 8, 64, 576), BF16),
            pltpu.VMEM((3, 4, 128), jnp.int32),
            pltpu.VMEM((HEADS, 512, 256), BF16),
            pltpu.VMEM((512, 2048), BF16),
            pltpu.VMEM((512, 2048), BF16),
            pltpu.VMEM((HEADS, 512, 256), F32),
        ),
        in_specs=[hbm] * 5,
        out_specs=(vmem,) * 6,
        scratch_shapes=[
            pltpu.VMEM((512, 3072), BF16),
            pltpu.VMEM((512, GROUP * 128), BF16),
            pltpu.VMEM((512, GROUP * 128), BF16),
            pltpu.VMEM((512, 128), BF16),
            pltpu.VMEM((512, 128), BF16),
            pltpu.SemaphoreType.DMA((2, 9)),
            pltpu.SemaphoreType.DMA((2, 9)),
            pltpu.SemaphoreType.DMA((8,)),
            pltpu.SemaphoreType.DMA((8,)),
            pltpu.SemaphoreType.DMA((3,)),
            pltpu.SemaphoreType.DMA((4,)),
            pltpu.SemaphoreType.DMA((5,)),
        ],
        compiler_params=pltpu.CompilerParams(collective_id=0, has_side_effects=True, vmem_limit_bytes=20 * 2**20),
    )(*operands)


def earlier_kernel(lat_ref, docs_ref, qp, wk_ref, wv_ref, acc_ref, out_ref, o_s, k_s, v_s, tail_s, rng_s, out_sem):
    def document(row):
        b, rest = divmod(row, 512)
        return docs_ref[b, rest // 128, rest % 128]

    def first_chunk(block):
        lowest = jnp.int32(4)
        for c in reversed(range(block, 4)):
            lowest = jnp.where(document(c * T + T - 1) == document(1024 + block * T), c, lowest)
        return lowest

    first, both = first_chunk(0), first_chunk(1) < 4
    lat = lat_ref.reshape(24, 64, 576)

    def tails(start, end):
        for r in range(start, end):
            rope = lat[2 * r:2 * r + 2, :, 512:].reshape(128, 64)
            tail_s[pl.ds(128 * r, 128), :] = key_tail(rope, docs_ref[r // 4, r % 4:r % 4 + 1, :])

    rng_s[0] = jnp.ones((T, 128), F32)
    rng_s[1] = jnp.ones((T, 128), F32)

    def store(g, h, row, acc):
        total = acc[:, 128:]
        o_s[g, pl.ds(row, acc.shape[0]), h * 128:(h + 1) * 128] = (acc[:, :128] / total).astype(BF16)
        for t in range(acc.shape[0] // T):
            rng_s[0] = jnp.minimum(rng_s[0], total[t * T:(t + 1) * T])
            rng_s[1] = jnp.maximum(rng_s[1], total[t * T:(t + 1) * T])

    def write(g):
        return pltpu.make_async_copy(o_s.at[g], out_ref.at[:, pl.ds(pl.multiple_of(g * GROUP * 128, 128), GROUP * 128)], out_sem.at[g])

    def run(start, reach):
        count = 4 - start
        if count:
            tails(2 * start, 8)

        def step(g, carry):
            columns = pl.ds(pl.multiple_of(g * GROUP * 128, 128), GROUP * 128)
            if count:
                latent = lat[4 * start:16, :, :512].reshape(count * T, 512)
                k_s[pl.ds(0, count * T), :] = expand(latent, wk_ref[:, columns])
                v_s[pl.ds(0, count * T), :] = expand(latent, wv_ref[:, columns])
            for h in range(GROUP):
                head = g * GROUP + h
                acc = acc_ref[head, pl.ds(0, reach), :]
                for c in range(count):
                    rows = pl.ds(c * T, T)
                    keys = jnp.concatenate([k_s[rows, h * 128:(h + 1) * 128], tail_s[pl.ds((start + c) * T, T), :]], axis=1)
                    weights = jnp.exp2(scores(qp[head, pl.ds(0, reach), :], keys)).astype(BF16)
                    acc = acc + jnp.dot(weights, with_ones(v_s[rows, h * 128:(h + 1) * 128]), preferred_element_type=F32)
                store(g, h, 0, acc)
                if reach < 512:
                    store(g, h, reach, acc_ref[head, pl.ds(reach, 512 - reach), :])
            write(g).start()
            return carry

        lax.fori_loop(0, HEADS // GROUP, step, 0)

    for start in range(5):
        for reach in ((512,) if start == 4 else (256,) if start == 0 else (256, 512)):
            chosen = first == start
            if start < 4:
                chosen = chosen & (both if reach == 512 else jnp.logical_not(both))
            pl.when(chosen)(functools.partial(run, start, reach))
    for g in range(HEADS // GROUP):
        write(g).wait()

    inside = (jnp.min(rng_s[0]) >= LOW) & (jnp.max(rng_s[1]) <= HIGH)

    @pl.when(jnp.logical_not(inside))
    def _():
        tails(0, 12)

        def group(g, carry):
            columns = pl.ds(pl.multiple_of(g * GROUP * 128, 128), GROUP * 128)

            def widen(c, carry):
                latent = lat[pl.ds(c * 4, 4), :, :512].reshape(T, 512)
                rows = pl.ds(pl.multiple_of(c * T, T), T)
                k_s[rows, :] = expand(latent, wk_ref[:, columns])
                v_s[rows, :] = expand(latent, wv_ref[:, columns])
                return carry

            lax.fori_loop(first, 6, widen, 0)
            causal = causal_mask()
            for h in range(GROUP):
                for qb in range(2):
                    end = 4 + qb

                    def body(c, state):
                        peak, acc = state
                        rows = pl.ds(pl.multiple_of(c * T, T), T)
                        keys = jnp.concatenate([k_s[rows, h * 128:(h + 1) * 128], tail_s[rows, :]], axis=1)
                        s = scores(qp[g * GROUP + h, pl.ds(qb * T, T), :], keys)
                        s = jnp.where(causal | (c < end), s, -BIG)
                        new = jnp.maximum(peak, jnp.max(s, axis=1, keepdims=True))
                        weights = jnp.exp2(s - new).astype(BF16)
                        t = jnp.dot(weights, with_ones(v_s[rows, h * 128:(h + 1) * 128]), preferred_element_type=F32)
                        return new, acc * jnp.exp2(peak - new) + t

                    initial = (jnp.full((T, 1), -BIG, F32), jnp.zeros((T, 256), F32))
                    _, acc = lax.fori_loop(first, end + 1, body, initial)
                    o_s[g, pl.ds(qb * T, T), h * 128:(h + 1) * 128] = (acc[:, :128] / acc[:, 128:]).astype(BF16)
            write(g).start()
            write(g).wait()
            return carry

        lax.fori_loop(0, HEADS // GROUP, group, 0)


def earlier(lat, docs, qp, w_key, w_value, acc):
    vmem, hbm = pl.BlockSpec(memory_space=pltpu.VMEM), pl.BlockSpec(memory_space=pltpu.HBM)
    return pl.pallas_call(
        earlier_kernel,
        out_shape=jax.ShapeDtypeStruct((512, 2048), BF16),
        in_specs=[vmem] * 6,
        out_specs=hbm,
        scratch_shapes=[
            pltpu.VMEM((HEADS // GROUP, 512, GROUP * 128), BF16),
            pltpu.VMEM((1536, GROUP * 128), BF16),
            pltpu.VMEM((1536, GROUP * 128), BF16),
            pltpu.VMEM((1536, 128), BF16),
            pltpu.VMEM((2, T, 128), F32),
            pltpu.SemaphoreType.DMA((HEADS // GROUP,)),
        ],
        compiler_params=pltpu.CompilerParams(vmem_limit_bytes=20 * 2**20),
    )(lat, docs, qp, w_key, w_value, acc)


def on_device(queries, latent_cache, doc_ids, w_key, w_value):
    lat, docs, qp, wk, wv, acc = gather(latent_cache, doc_ids.reshape(4, 128), queries, w_key, w_value)
    return earlier(lat, docs, qp, wk, wv, acc)


def solution(mesh):
    placed = (P("ctx", "dp"), P(("ctx", "dp"), None), P("ctx"), P(None, "dp"), P(None, "dp"))
    return jax.shard_map(on_device, mesh=mesh, in_specs=placed, out_specs=P("ctx", "dp"), check_vma=False)
```

time: 352 us -> 137 us (0.39)
  the two profiles are of different devices: /device:TPU:16 before, /device:TPU:25 now
where the time goes in v2:
time: 137 us
  Pallas kernels  137 us (100%)
    pallas_call x1, Pallas kernels, earlier(): pl.pallas_call(earlier_kernel, out_shape=jax.ShapeDtypeStruct((512, 2048)...  110 us
    pallas_call x1, Pallas kernels, gather(): pl.pallas_call(gather_kernel, out_shape=(pltpu.VMEM((3, 8, 64, 576), BF16...  26.2 us

profile of v2, /device:TPU:25, one launch (start us, length us, event | category | flops | bytes accessed | tf_op | source)
XLA Modules:
  0.0 136.8 jit_solution(16386164741449068335)
XLA Ops:
  0.0 26.2 %shard_map.55 = (bf16[3,8,64,576]{3,2,1,0:T(8,128)(2,1)S(1)}, s32[3,4,128]{2,1,0:T(4,128)S(1)}, bf16[16,512,256]{2,1,0:T(8,128)(2,1)S(1)}, bf16[512,2048]{1,0:T(...) custom-call(bf16[64,576]{1,0:T(8,128)(2,1)} %lat_ref.1, s32[4,128]{1,0:T(4,128)} %bitcast.1, ...), custom_call_target="tpu_custom_call" | custom-call | tf_op jit(solution)/shard_map/pallas_call | solution.py:256
  26.2 110.4 %shard_map.56 = bf16[512,2048]{1,0:T(8,128)(2,1)} custom-call(bf16[3,8,64,576]{3,2,1,0:T(8,128)(2,1)S(1)} %get-tuple-element.11.lat_ref, s32[3,4,128]{2,1,0:T(4,128)S(1)} %get-tuple-element.12.docs_ref, bf16[16,512,256]{2,1,0:T(8,128)(2,1)S(1)} %get-tuple-element.13.qp, bf16[512,2048]{1,0:T(8,128)(2,1)S(1)} %get-tuple-element.14.wk_ref, ...), custom_call_target="tpu_custom_call" | custom-call | tf_op jit(solution)/shard_map/pallas_call | solution.py:399

commit v3 on v2

--- a/solution.py
+++ b/solution.py
@@ -51,9 +51,18 @@
     return lax.broadcasted_iota(jnp.int32, (T, T), 1) <= lax.broadcasted_iota(jnp.int32, (T, T), 0)
 
 
+def rows_of(window, shards):
+    return jnp.concatenate([window[k, :, 512 * j:512 * j + 512] for k in shards for j in range(2)], axis=0)
+
+
+def rope_of(window, shards):
+    packed = [window[k, :, 1024:] for k in shards]
+    return jnp.concatenate([p[:, 64 * j:64 * j + 64] for p in packed for j in range(2)], axis=0)
+
+
 def gather_kernel(lat_ref, docs_ref, q_ref, wk_ref, wv_ref,
-                  lat_s, docs_s, qp, wk_s, wv_s, acc_s,
-                  q_s, k_s, v_s, tail_s, qtail_s,
+                  win, docs_s, qp, wk_s, wv_s, acc_s,
+                  lat_s, own_s, q_s, k_s, v_s, tail_s, qtail_s,
                   send, recv, relay_send, relay_recv, misc_send, misc_recv, load_sem):
     ctx, dp = lax.axis_index("ctx"), lax.axis_index("dp")
     x, y, core = dp // 2, dp % 2, ctx % 2
@@ -66,27 +75,30 @@
     shard = [column * 2 + row for column in (x, left_x, right_x, far_x) for row in (y, 1 - y)]
 
     barrier = pltpu.get_barrier_semaphore()
-    for peer in (partner, right, left, next1, next2, prev1, prev2):
+
+    def greet(peer):
         pl.semaphore_signal(barrier, inc=1, device_id=peer, device_id_type=MESH)
 
+    for peer in (partner, right, left):
+        greet(peer)
+    pl.when(ctx >= 1)(lambda: greet(prev1))
+    pl.when(ctx >= 2)(lambda: greet(prev2))
+    pl.when(core == 0)(lambda: greet(sibling))
+
     loads = [pltpu.make_async_copy(src, dst, load_sem.at[i]) for i, (src, dst) in enumerate((
-        (lat_ref, lat_s.at[2, dp]), (docs_ref, docs_s.at[2]), (q_ref, q_s), (wk_ref, wk_s), (wv_ref, wv_s)))]
+        (lat_ref, lat_s), (docs_ref, docs_s.at[2]), (q_ref, q_s), (wk_ref, wk_s), (wv_ref, wv_s)))]
     for c in loads:
         c.start()
-    pl.semaphore_wait(barrier, 7)
 
     def remote(src, dst, send_sem, recv_sem, peer):
         return pltpu.make_async_remote_copy(
             src_ref=src, dst_ref=dst, send_sem=send_sem, recv_sem=recv_sem, device_id=peer, device_id_type=MESH)
 
     def piece(w, k, half=None):
-        block = lat_s.at[2 * w, shard[k]]
-        return block if half is None else block.at[pl.ds(32 * half, 32)]
-
-    brings = {
-        1: [(1, None), (2, None), (3, None), (4, None), (5, None), (6, 0), (7, 0), (6, 1), (7, 1)],
-        0: [(1, None), (2, None), (4, None), (6, 0), (6, 1), (3, None), (5, None), (7, None)],
-    }
+        block = win.at[2 * w, shard[k]]
+        return block if half is None else block.at[pl.ds(16 * half, 16)]
+
+    brings = [(1, None), (2, None), (3, None), (4, None), (5, None), (6, 0), (7, 0), (6, 1), (7, 1)]
     started = []
 
     def go(w, slot, src, dst, peer):
@@ -95,63 +107,60 @@
         started.append(c)
 
     def got(w, slot):
-        place = piece(w, *brings[w][slot])
+        place = piece(w, *brings[slot])
         remote(place, place, send.at[w, slot], recv.at[w, slot], partner).wait_recv()
 
-    def same(w, slot, k, peer, half=None):
+    def pass_on(w, slot, k, peer, half=None):
         go(w, slot, piece(w, k, half), piece(w, k, half), peer)
 
     def relay(k):
-        return remote(lat_s.at[2 - 2 * core, shard[k]], lat_s.at[1, shard[k]], relay_send.at[k], relay_recv.at[k], sibling)
+        return remote(win.at[2 - 2 * core, shard[k]], win.at[1, shard[k]], relay_send.at[k], relay_recv.at[k], sibling)
 
     def relay_if(w, k):
         @pl.when(core == 1 - w)
         def _():
             relay(k).start()
 
-    onward = remote(lat_ref, lat_s.at[0, dp], misc_send.at[0], misc_recv.at[0], next2)
-    stay = pltpu.make_async_copy(lat_ref, lat_s.at[0, dp], misc_recv.at[3])
-    d1 = remote(docs_ref, docs_s.at[1], misc_send.at[1], misc_recv.at[1], next1)
-    d2 = remote(docs_ref, docs_s.at[0], misc_send.at[2], misc_recv.at[2], next2)
-
-    go(1, 0, lat_ref, piece(1, 0), partner)
-    go(1, 1, lat_ref, piece(1, 0), right)
-    go(1, 3, lat_ref, piece(1, 0), left)
-
-    @pl.when(ctx < 14)
-    def _():
-        onward.start()
-
-    @pl.when(ctx < 2)
-    def _():
-        stay.start()
-
-    d1.start()
-    d2.start()
     loads[0].wait()
-    relay_if(1, 0)
-
-    got(1, 0)
-    same(1, 2, 1, right)
-    same(1, 4, 1, left)
-    relay_if(1, 1)
-
-    @pl.when(ctx >= 2)
-    def _():
-        onward.wait_recv()
-
-    @pl.when(ctx < 2)
-    def _():
-        stay.wait()
-
-    same(0, 1, 0, right)
-    same(0, 2, 0, left)
-    same(0, 0, 0, partner)
-    relay_if(0, 0)
+    packed = jnp.concatenate(
+        [lat_s[:32, :512], lat_s[32:, :512], lat_s[:32, 512:], lat_s[32:, 512:]], axis=1)
+    own_s[...] = packed
+    win[2, dp] = packed
 
     loads[1].wait()
     for r in range(4):
         qtail_s[pl.ds(128 * r, 128), :] = query_tail(docs_s[2, r:r + 1, :])
+
+    @pl.when(ctx < 2)
+    def _():
+        docs_s[0] = jnp.full((4, 128), -1, jnp.int32)
+        win[0, dp] = packed
+
+    @pl.when(ctx < 1)
+    def _():
+        docs_s[1] = jnp.full((4, 128), -1, jnp.int32)
+
+    onward = remote(own_s, win.at[0, dp], misc_send.at[0], misc_recv.at[0], next2)
+    d1 = remote(docs_ref, docs_s.at[1], misc_send.at[1], misc_recv.at[1], next1)
+    d2 = remote(docs_ref, docs_s.at[0], misc_send.at[2], misc_recv.at[2], next2)
+
+    pl.semaphore_wait(barrier, 3 + jnp.where(ctx < 15, 1, 0) + jnp.where(ctx < 14, 1, 0) + core)
+
+    go(1, 0, own_s, piece(1, 0), partner)
+    go(1, 1, own_s, piece(1, 0), right)
+    go(1, 3, own_s, piece(1, 0), left)
+
+    @pl.when(ctx < 14)
+    def _():
+        onward.start()
+        d2.start()
+
+    @pl.when(ctx < 15)
+    def _():
+        d1.start()
+
+    relay_if(1, 0)
+
     loads[2].wait()
     qtail = qtail_s[...]
 
@@ -165,50 +174,73 @@
 
     lax.fori_loop(0, HEADS // 2, prepare, 0)
 
+    got(1, 0)
+    pass_on(1, 2, 1, right)
+    pass_on(1, 4, 1, left)
+    relay_if(1, 1)
     got(1, 1)
-    same(1, 5, 2, right, 0)
+    pass_on(1, 5, 2, right, 0)
+    got(1, 3)
+    pass_on(1, 7, 4, left, 1)
     relay_if(1, 2)
-    got(1, 3)
-    same(1, 7, 4, left, 1)
     relay_if(1, 4)
+
+    @pl.when(ctx >= 2)
+    def _():
+        onward.wait_recv()
+
+    pass_on(0, 0, 0, partner)
+    relay_if(0, 0)
+
+    loads[3].wait()
+    loads[4].wait()
+
+    def widen(kinds):
+        latent = rows_of(win.at[2], [shard[k] for k in kinds])
+
+        def some(g, carry):
+            columns = pl.ds(pl.multiple_of(g * 512, 512), 512)
+            for weight, out in ((wk_s, k_s), (wv_s, v_s)):
+                wide = expand(latent, weight[:, columns])
+                for i, k in enumerate(kinds):
+                    out[pl.ds(pl.multiple_of(shard[k] * 64, 64), 64), columns] = wide[64 * i:64 * i + 64]
+            return carry
+
+        lax.fori_loop(0, 4, some, 0)
+
+    widen((0, 1, 2, 4))
+
     got(1, 2)
-    same(1, 6, 3, right, 0)
+    pass_on(1, 6, 3, right, 0)
+    got(1, 4)
+    pass_on(1, 8, 5, left, 1)
+    pass_on(0, 1, 0, right)
+    pass_on(0, 3, 0, left)
     relay_if(1, 3)
-    got(1, 4)
-    same(1, 8, 5, left, 1)
     relay_if(1, 5)
-    got(0, 1)
-    same(0, 3, 2, right, 0)
-    same(0, 5, 2, partner)
-    relay_if(0, 2)
-    got(0, 2)
-    same(0, 4, 4, left, 1)
-    same(0, 6, 4, partner)
-    relay_if(0, 4)
+    got(0, 0)
+    pass_on(0, 2, 1, right)
+    pass_on(0, 4, 1, left)
+    relay_if(0, 1)
     got(1, 5)
     got(1, 7)
     relay_if(1, 6)
     got(1, 6)
     got(1, 8)
     relay_if(1, 7)
-
-    loads[3].wait()
-    loads[4].wait()
+    widen((3, 5, 6, 7))
+
     for r in range(4):
-        rope = lat_s[2, 2 * r:2 * r + 2, :, 512:].reshape(128, 64)
-        tail_s[pl.ds(128 * r, 128), :] = key_tail(rope, docs_s[2, r:r + 1, :])
+        tail_s[pl.ds(128 * r, 128), :] = key_tail(rope_of(win.at[2], (2 * r, 2 * r + 1)), docs_s[2, r:r + 1, :])
 
     def own(g, carry):
-        columns = pl.ds(pl.multiple_of(g * GROUP * 128, 128), GROUP * 128)
-        latent = lat_s[2, :, :, :512].reshape(512, 512)
-        k_s[...] = expand(latent, wk_s[:, columns])
-        v_s[...] = expand(latent, wv_s[:, columns])
         causal = causal_mask()
         tail = tail_s[...]
         for h in range(GROUP):
             head = g * GROUP + h
-            keys = jnp.concatenate([k_s[:, h * 128:(h + 1) * 128], tail], axis=1)
-            value = with_ones(v_s[:, h * 128:(h + 1) * 128])
+            columns = pl.ds(pl.multiple_of(head * 128, 128), 128)
+            keys = jnp.concatenate([k_s[:, columns], tail], axis=1)
+            value = with_ones(v_s[:, columns])
             for qb in range(2):
                 s = scores(qp[head, pl.ds(qb * T, T), :], keys[:(qb + 1) * T])
                 diagonal = jnp.where(causal, s[:, qb * T:], -BIG)
@@ -218,36 +250,52 @@
         return carry
 
     lax.fori_loop(0, 1, own, 0)
+    got(0, 1)
+    pass_on(0, 5, 2, right, 0)
     got(0, 3)
+    pass_on(0, 7, 4, left, 1)
+    relay_if(0, 2)
+    relay_if(0, 4)
+    lax.fori_loop(1, 2, own, 0)
+    got(0, 2)
+    pass_on(0, 6, 3, right, 0)
     got(0, 4)
-    same(0, 7, 6, partner)
+    pass_on(0, 8, 5, left, 1)
+    relay_if(0, 3)
+    relay_if(0, 5)
+    lax.fori_loop(2, 3, own, 0)
+    got(0, 5)
+    got(0, 7)
     relay_if(0, 6)
-    got(0, 0)
-    relay_if(0, 1)
-    got(0, 5)
-    relay_if(0, 3)
     got(0, 6)
-    relay_if(0, 5)
-    lax.fori_loop(1, 2, own, 0)
-    got(0, 7)
+    got(0, 8)
     relay_if(0, 7)
-    lax.fori_loop(2, HEADS // GROUP, own, 0)
-
-    d1.wait_recv()
-    d2.wait_recv()
+    lax.fori_loop(3, HEADS // GROUP, own, 0)
+
+    @pl.when(ctx >= 1)
+    def _():
+        d1.wait_recv()
+
+    @pl.when(ctx >= 2)
+    def _():
+        d2.wait_recv()
+
     for k in range(8):
-        place = lat_s.at[1, shard[k]]
+        place = win.at[1, shard[k]]
         remote(place, place, relay_send.at[k], relay_recv.at[k], sibling).wait_recv()
     for c in started:
         c.wait_send()
     for k in range(8):
         relay(k).wait_send()
-    d1.wait_send()
-    d2.wait_send()
 
     @pl.when(ctx < 14)
     def _():
         onward.wait_send()
+        d2.wait_send()
+
+    @pl.when(ctx < 15)
+    def _():
+        d1.wait_send()
 
 
 def gather(latent, docs, queries, w_key, w_value):
@@ -256,7 +304,7 @@
     return pl.pallas_call(
         gather_kernel,
         out_shape=(
-            pltpu.VMEM((3, 8, 64, 576), BF16),
+            pltpu.VMEM((3, 8, 32, 1152), BF16),
             pltpu.VMEM((3, 4, 128), jnp.int32),
             pltpu.VMEM((HEADS, 512, 256), BF16),
             pltpu.VMEM((512, 2048), BF16),
@@ -266,9 +314,11 @@
         in_specs=[hbm] * 5,
         out_specs=(vmem,) * 6,
         scratch_shapes=[
+            pltpu.VMEM((64, 576), BF16),
+            pltpu.VMEM((32, 1152), BF16),
             pltpu.VMEM((512, 3072), BF16),
-            pltpu.VMEM((512, GROUP * 128), BF16),
-            pltpu.VMEM((512, GROUP * 128), BF16),
+            pltpu.VMEM((512, HEADS * 128), BF16),
+            pltpu.VMEM((512, HEADS * 128), BF16),
             pltpu.VMEM((512, 128), BF16),
             pltpu.VMEM((512, 128), BF16),
             pltpu.SemaphoreType.DMA((2, 9)),
@@ -276,14 +326,14 @@
             pltpu.SemaphoreType.DMA((8,)),
             pltpu.SemaphoreType.DMA((8,)),
             pltpu.SemaphoreType.DMA((3,)),
-            pltpu.SemaphoreType.DMA((4,)),
+            pltpu.SemaphoreType.DMA((3,)),
             pltpu.SemaphoreType.DMA((5,)),
         ],
         compiler_params=pltpu.CompilerParams(collective_id=0, has_side_effects=True, vmem_limit_bytes=20 * 2**20),
     )(*operands)
 
 
-def earlier_kernel(lat_ref, docs_ref, qp, wk_ref, wv_ref, acc_ref, out_ref, o_s, k_s, v_s, tail_s, rng_s, out_sem):
+def earlier_kernel(win_ref, docs_ref, qp, wk_ref, wv_ref, acc_ref, out_ref, o_s, k_s, v_s, tail_s, rng_s, out_sem):
     def document(row):
         b, rest = divmod(row, 512)
         return docs_ref[b, rest // 128, rest % 128]
@@ -295,11 +345,11 @@
         return lowest
 
     first, both = first_chunk(0), first_chunk(1) < 4
-    lat = lat_ref.reshape(24, 64, 576)
+    window = win_ref.reshape(24, 32, 1152)
 
     def tails(start, end):
         for r in range(start, end):
-            rope = lat[2 * r:2 * r + 2, :, 512:].reshape(128, 64)
+            rope = rope_of(window, (2 * r, 2 * r + 1))
             tail_s[pl.ds(128 * r, 128), :] = key_tail(rope, docs_ref[r // 4, r % 4:r % 4 + 1, :])
 
     rng_s[0] = jnp.ones((T, 128), F32)
@@ -323,7 +373,7 @@
         def step(g, carry):
             columns = pl.ds(pl.multiple_of(g * GROUP * 128, 128), GROUP * 128)
             if count:
-                latent = lat[4 * start:16, :, :512].reshape(count * T, 512)
+                latent = rows_of(window, range(4 * start, 16))
                 k_s[pl.ds(0, count * T), :] = expand(latent, wk_ref[:, columns])
                 v_s[pl.ds(0, count * T), :] = expand(latent, wv_ref[:, columns])
             for h in range(GROUP):
@@ -361,7 +411,7 @@
             columns = pl.ds(pl.multiple_of(g * GROUP * 128, 128), GROUP * 128)
 
             def widen(c, carry):
-                latent = lat[pl.ds(c * 4, 4), :, :512].reshape(T, 512)
+                latent = rows_of(window, [4 * c + i for i in range(4)])
                 rows = pl.ds(pl.multiple_of(c * T, T), T)
                 k_s[rows, :] = expand(latent, wk_ref[:, columns])
                 v_s[rows, :] = expand(latent, wv_ref[:, columns])
@@ -394,7 +444,7 @@
         lax.fori_loop(0, HEADS // GROUP, group, 0)
 
 
-def earlier(lat, docs, qp, w_key, w_value, acc):
+def earlier(window, docs, qp, w_key, w_value, acc):
     vmem, hbm = pl.BlockSpec(memory_space=pltpu.VMEM), pl.BlockSpec(memory_space=pltpu.HBM)
     return pl.pallas_call(
         earlier_kernel,
@@ -410,12 +460,12 @@
             pltpu.SemaphoreType.DMA((HEADS // GROUP,)),
         ],
         compiler_params=pltpu.CompilerParams(vmem_limit_bytes=20 * 2**20),
-    )(lat, docs, qp, w_key, w_value, acc)
+    )(window, docs, qp, w_key, w_value, acc)
 
 
 def on_device(queries, latent_cache, doc_ids, w_key, w_value):
-    lat, docs, qp, wk, wv, acc = gather(latent_cache, doc_ids.reshape(4, 128), queries, w_key, w_value)
-    return earlier(lat, docs, qp, wk, wv, acc)
+    window, docs, qp, wk, wv, acc = gather(latent_cache, doc_ids.reshape(4, 128), queries, w_key, w_value)
+    return earlier(window, docs, qp, wk, wv, acc)
 
 
 def solution(mesh):

time: 137 us -> 120 us (0.88)
  the two profiles are of different devices: /device:TPU:25 before, /device:TPU:32 now
where the time goes in v3:
time: 120 us
  Pallas kernels  120 us (100%)
    pallas_call x1, Pallas kernels, earlier(): pl.pallas_call(earlier_kernel, out_shape=jax.ShapeDtypeStruct((512, 2048)...  94.9 us
    pallas_call x1, Pallas kernels, gather(): pl.pallas_call(gather_kernel, out_shape=(pltpu.VMEM((3, 8, 32, 1152), BF1...  25.1 us

profile of v3, /device:TPU:32, one launch (start us, length us, event | category | flops | bytes accessed | tf_op | source)
XLA Modules:
  0.0 120.1 jit_solution(2633616438176116288)
XLA Ops:
  0.0 25.1 %shard_map.55 = (bf16[3,8,32,1152]{3,2,1,0:T(8,128)(2,1)S(1)}, s32[3,4,128]{2,1,0:T(4,128)S(1)}, bf16[16,512,256]{2,1,0:T(8,128)(2,1)S(1)}, bf16[512,2048]{1,0:T...) custom-call(bf16[64,576]{1,0:T(8,128)(2,1)} %lat_ref.1, s32[4,128]{1,0:T(4,128)} %bitcast.1, ...), custom_call_target="tpu_custom_call" | custom-call | tf_op jit(solution)/shard_map/pallas_call | solution.py:304
  25.1 94.9 %shard_map.56 = bf16[512,2048]{1,0:T(8,128)(2,1)} custom-call(bf16[3,8,32,1152]{3,2,1,0:T(8,128)(2,1)S(1)} %get-tuple-element.11.win_ref, s32[3,4,128]{2,1,0:T(4,128)S(1)} %get-tuple-element.12.docs_ref, bf16[16,512,256]{2,1,0:T(8,128)(2,1)S(1)} %get-tuple-element.13.qp, bf16[512,2048]{1,0:T(8,128)(2,1)S(1)} %get-tuple-element.14.wk_ref, ...), custom_call_target="tpu_custom_call" | custom-call | tf_op jit(solution)/shard_map/pallas_call | solution.py:449

commit v4 on v3

--- a/solution.py
+++ b/solution.py
@@ -67,20 +67,26 @@
     ctx, dp = lax.axis_index("ctx"), lax.axis_index("dp")
     x, y, core = dp // 2, dp % 2, ctx % 2
     right_x, left_x, far_x = (x + 1) % 4, (x + 3) % 4, (x + 2) % 4
-    partner = (ctx, x * 2 + 1 - y)
-    right, left = (ctx, right_x * 2 + y), (ctx, left_x * 2 + y)
     next1, next2 = ((ctx + 1) % 16, dp), ((ctx + 2) % 16, dp)
     prev1, prev2 = ((ctx + 15) % 16, dp), ((ctx + 14) % 16, dp)
     sibling = (ctx + 1 - 2 * core, dp)
+    peers = {
+        "partner": (ctx, x * 2 + 1 - y), "right": (ctx, right_x * 2 + y), "left": (ctx, left_x * 2 + y),
+        "far": (ctx, far_x * 2 + y), "next": next2}
+    turn = ctx // 2 == 4
+    before_turn = ctx // 2 == 3
     shard = [column * 2 + row for column in (x, left_x, right_x, far_x) for row in (y, 1 - y)]
+    kind_there = {
+        "partner": lambda k: k ^ 1, "right": lambda k: 2 + k, "left": lambda k: 4 + k, "far": lambda k: 6 + k,
+        "next": lambda k: k}
 
     barrier = pltpu.get_barrier_semaphore()
 
     def greet(peer):
         pl.semaphore_signal(barrier, inc=1, device_id=peer, device_id_type=MESH)
 
-    for peer in (partner, right, left):
-        greet(peer)
+    for name in ("partner", "right", "left", "far"):
+        greet(peers[name])
     pl.when(ctx >= 1)(lambda: greet(prev1))
     pl.when(ctx >= 2)(lambda: greet(prev2))
     pl.when(core == 0)(lambda: greet(sibling))
@@ -94,32 +100,29 @@
         return pltpu.make_async_remote_copy(
             src_ref=src, dst_ref=dst, send_sem=send_sem, recv_sem=recv_sem, device_id=peer, device_id_type=MESH)
 
-    def piece(w, k, half=None):
-        block = win.at[2 * w, shard[k]]
-        return block if half is None else block.at[pl.ds(16 * half, 16)]
-
-    brings = [(1, None), (2, None), (3, None), (4, None), (5, None), (6, 0), (7, 0), (6, 1), (7, 1)]
+    def piece(w, k):
+        return win.at[2 * w, shard[k]]
+
     started = []
 
-    def go(w, slot, src, dst, peer):
-        c = remote(src, dst, send.at[w, slot], recv.at[w, slot], peer)
-        c.start()
-        started.append(c)
-
-    def got(w, slot):
-        place = piece(w, *brings[slot])
-        remote(place, place, send.at[w, slot], recv.at[w, slot], partner).wait_recv()
-
-    def pass_on(w, slot, k, peer, half=None):
-        go(w, slot, piece(w, k, half), piece(w, k, half), peer)
+    def give(w, k, where, condition=None):
+        to = 0 if where == "next" else w
+        src = own_s if (w, k) == (1, 0) else piece(w, k)
+        c = remote(src, win.at[2 * to, shard[k]], send.at[len(started)], recv.at[to, kind_there[where](k)], peers[where])
+        started.append((c, condition))
+        if condition is None:
+            c.start()
+        else:
+            pl.when(condition)(c.start)
+
+    def got(w, k):
+        remote(piece(w, k), piece(w, k), send.at[0], recv.at[w, k], sibling).wait_recv()
 
     def relay(k):
         return remote(win.at[2 - 2 * core, shard[k]], win.at[1, shard[k]], relay_send.at[k], relay_recv.at[k], sibling)
 
     def relay_if(w, k):
-        @pl.when(core == 1 - w)
-        def _():
-            relay(k).start()
+        pl.when(core == 1 - w)(lambda: relay(k).start())
 
     loads[0].wait()
     packed = jnp.concatenate(
@@ -134,31 +137,23 @@
     @pl.when(ctx < 2)
     def _():
         docs_s[0] = jnp.full((4, 128), -1, jnp.int32)
-        win[0, dp] = packed
+        for k in (0, 2, 4, 6):
+            win[0, shard[k]] = packed
 
     @pl.when(ctx < 1)
     def _():
         docs_s[1] = jnp.full((4, 128), -1, jnp.int32)
 
-    onward = remote(own_s, win.at[0, dp], misc_send.at[0], misc_recv.at[0], next2)
-    d1 = remote(docs_ref, docs_s.at[1], misc_send.at[1], misc_recv.at[1], next1)
-    d2 = remote(docs_ref, docs_s.at[0], misc_send.at[2], misc_recv.at[2], next2)
-
-    pl.semaphore_wait(barrier, 3 + jnp.where(ctx < 15, 1, 0) + jnp.where(ctx < 14, 1, 0) + core)
-
-    go(1, 0, own_s, piece(1, 0), partner)
-    go(1, 1, own_s, piece(1, 0), right)
-    go(1, 3, own_s, piece(1, 0), left)
-
-    @pl.when(ctx < 14)
-    def _():
-        onward.start()
-        d2.start()
-
-    @pl.when(ctx < 15)
-    def _():
-        d1.start()
-
+    d1 = remote(docs_ref, docs_s.at[1], misc_send.at[0], misc_recv.at[0], next1)
+    d2 = remote(docs_ref, docs_s.at[0], misc_send.at[1], misc_recv.at[1], next2)
+
+    pl.semaphore_wait(barrier, 4 + jnp.where(ctx < 15, 1, 0) + jnp.where(ctx < 14, 1, 0) + core)
+
+    for where in ("partner", "right", "left", "far"):
+        give(1, 0, where)
+    give(1, 0, "next", ctx < 14)
+    pl.when(ctx < 14)(d2.start)
+    pl.when(ctx < 15)(d1.start)
     relay_if(1, 0)
 
     loads[2].wait()
@@ -174,27 +169,6 @@
 
     lax.fori_loop(0, HEADS // 2, prepare, 0)
 
-    got(1, 0)
-    pass_on(1, 2, 1, right)
-    pass_on(1, 4, 1, left)
-    relay_if(1, 1)
-    got(1, 1)
-    pass_on(1, 5, 2, right, 0)
-    got(1, 3)
-    pass_on(1, 7, 4, left, 1)
-    relay_if(1, 2)
-    relay_if(1, 4)
-
-    @pl.when(ctx >= 2)
-    def _():
-        onward.wait_recv()
-
-    pass_on(0, 0, 0, partner)
-    relay_if(0, 0)
-
-    loads[3].wait()
-    loads[4].wait()
-
     def widen(kinds):
         latent = rows_of(win.at[2], [shard[k] for k in kinds])
 
@@ -207,31 +181,6 @@
             return carry
 
         lax.fori_loop(0, 4, some, 0)
-
-    widen((0, 1, 2, 4))
-
-    got(1, 2)
-    pass_on(1, 6, 3, right, 0)
-    got(1, 4)
-    pass_on(1, 8, 5, left, 1)
-    pass_on(0, 1, 0, right)
-    pass_on(0, 3, 0, left)
-    relay_if(1, 3)
-    relay_if(1, 5)
-    got(0, 0)
-    pass_on(0, 2, 1, right)
-    pass_on(0, 4, 1, left)
-    relay_if(0, 1)
-    got(1, 5)
-    got(1, 7)
-    relay_if(1, 6)
-    got(1, 6)
-    got(1, 8)
-    relay_if(1, 7)
-    widen((3, 5, 6, 7))
-
-    for r in range(4):
-        tail_s[pl.ds(128 * r, 128), :] = key_tail(rope_of(win.at[2], (2 * r, 2 * r + 1)), docs_s[2, r:r + 1, :])
 
     def own(g, carry):
         causal = causal_mask()
@@ -249,53 +198,84 @@
                 acc_s[head, pl.ds(qb * T, T), :] = jnp.dot(weights, value[:(qb + 1) * T], preferred_element_type=F32)
         return carry
 
-    lax.fori_loop(0, 1, own, 0)
-    got(0, 1)
-    pass_on(0, 5, 2, right, 0)
-    got(0, 3)
-    pass_on(0, 7, 4, left, 1)
-    relay_if(0, 2)
-    relay_if(0, 4)
-    lax.fori_loop(1, 2, own, 0)
-    got(0, 2)
-    pass_on(0, 6, 3, right, 0)
-    got(0, 4)
-    pass_on(0, 8, 5, left, 1)
-    relay_if(0, 3)
-    relay_if(0, 5)
-    lax.fori_loop(2, 3, own, 0)
-    got(0, 5)
-    got(0, 7)
-    relay_if(0, 6)
-    got(0, 6)
-    got(0, 8)
-    relay_if(0, 7)
-    lax.fori_loop(3, HEADS // GROUP, own, 0)
-
-    @pl.when(ctx >= 1)
-    def _():
-        d1.wait_recv()
-
-    @pl.when(ctx >= 2)
-    def _():
-        d2.wait_recv()
-
+    def owns(g):
+        lax.fori_loop(g, g + 1, own, 0)
+
+    forward = (ctx < 14) & jnp.logical_not(before_turn)
+
+    def earlier_shard(k):
+        pl.when(ctx >= 2)(lambda: got(0, k))
+        c = remote(piece(0, k), piece(0, k), send.at[40 + k], recv.at[0, k ^ 1], peers["partner"])
+        c.start()
+        relay_if(0, k)
+
+    def in_time(k):
+        pl.when(jnp.logical_not(turn))(lambda: earlier_shard(k))
+
+    def late(k):
+        pl.when(turn)(lambda: earlier_shard(k))
+
+    got(1, 1)
+    for where in ("right", "left", "far"):
+        give(1, 1, where)
+    relay_if(1, 1)
+    got(1, 2)
+    give(1, 2, "next", forward)
+    got(1, 4)
+    give(1, 4, "next", forward)
+    relay_if(1, 2)
+    relay_if(1, 4)
+    in_time(0)
+    loads[3].wait()
+    loads[4].wait()
+    widen((0, 1, 2, 4))
+    late(0)
+    for where in ("right", "left", "far"):
+        give(0, 0, where, turn)
+    got(1, 6)
+    give(1, 6, "next", forward)
+    relay_if(1, 6)
+    in_time(2)
+    got(1, 3)
+    relay_if(1, 3)
+    got(1, 5)
+    relay_if(1, 5)
+    in_time(4)
+    got(1, 7)
+    relay_if(1, 7)
+    widen((3, 5, 6, 7))
+    for r in range(4):
+        tail_s[pl.ds(128 * r, 128), :] = key_tail(rope_of(win.at[2], (2 * r, 2 * r + 1)), docs_s[2, r:r + 1, :])
+    late(2)
+    late(4)
+    owns(0)
+    earlier_shard(6)
+    owns(1)
+    for k in (1, 3):
+        got(0, k)
+        relay_if(0, k)
+    owns(2)
+    for k in (5, 7):
+        got(0, k)
+        relay_if(0, k)
+    owns(3)
+
+    pl.when(ctx >= 1)(d1.wait_recv)
+    pl.when(ctx >= 2)(d2.wait_recv)
     for k in range(8):
         place = win.at[1, shard[k]]
         remote(place, place, relay_send.at[k], relay_recv.at[k], sibling).wait_recv()
-    for c in started:
-        c.wait_send()
+    for c, condition in started:
+        if condition is None:
+            c.wait_send()
+        else:
+            pl.when(condition)(c.wait_send)
+    for k in (0, 2, 4, 6):
+        remote(piece(0, k), piece(0, k), send.at[40 + k], recv.at[0, k ^ 1], peers["partner"]).wait_send()
     for k in range(8):
         relay(k).wait_send()
-
-    @pl.when(ctx < 14)
-    def _():
-        onward.wait_send()
-        d2.wait_send()
-
-    @pl.when(ctx < 15)
-    def _():
-        d1.wait_send()
+    pl.when(ctx < 14)(d2.wait_send)
+    pl.when(ctx < 15)(d1.wait_send)
 
 
 def gather(latent, docs, queries, w_key, w_value):
@@ -321,12 +301,12 @@
             pltpu.VMEM((512, HEADS * 128), BF16),
             pltpu.VMEM((512, 128), BF16),
             pltpu.VMEM((512, 128), BF16),
-            pltpu.SemaphoreType.DMA((2, 9)),
-            pltpu.SemaphoreType.DMA((2, 9)),
+            pltpu.SemaphoreType.DMA((48,)),
+            pltpu.SemaphoreType.DMA((2, 8)),
             pltpu.SemaphoreType.DMA((8,)),
             pltpu.SemaphoreType.DMA((8,)),
-            pltpu.SemaphoreType.DMA((3,)),
-            pltpu.SemaphoreType.DMA((3,)),
+            pltpu.SemaphoreType.DMA((2,)),
+            pltpu.SemaphoreType.DMA((2,)),
             pltpu.SemaphoreType.DMA((5,)),
         ],
         compiler_params=pltpu.CompilerParams(collective_id=0, has_side_effects=True, vmem_limit_bytes=20 * 2**20),

time: 120 us -> 132 us (1.10)
  the two profiles are of different devices: /device:TPU:32 before, /device:TPU:17 now
where the time goes in v4:
time: 132 us
  Pallas kernels  131 us (99%)
    pallas_call x1, Pallas kernels, earlier(): pl.pallas_call(earlier_kernel, out_shape=jax.ShapeDtypeStruct((512, 2048)...  111 us
    pallas_call x1, Pallas kernels, gather(): pl.pallas_call(gather_kernel, out_shape=(pltpu.VMEM((3, 8, 32, 1152), BF1...  20.8 us

profile of v4, /device:TPU:17, one launch (start us, length us, event | category | flops | bytes accessed | tf_op | source)
XLA Modules:
  0.0 131.6 jit_solution(15323252025368970251)
XLA Ops:
  0.0 20.8 %shard_map.55 = (bf16[3,8,32,1152]{3,2,1,0:T(8,128)(2,1)S(1)}, s32[3,4,128]{2,1,0:T(4,128)S(1)}, bf16[16,512,256]{2,1,0:T(8,128)(2,1)S(1)}, bf16[512,2048]{1,0:T...) custom-call(bf16[64,576]{1,0:T(8,128)(2,1)} %lat_ref.1, s32[4,128]{1,0:T(4,128)} %bitcast.1, ...), custom_call_target="tpu_custom_call" | custom-call | tf_op jit(solution)/shard_map/pallas_call | solution.py:284
  20.8 110.7 %shard_map.56 = bf16[512,2048]{1,0:T(8,128)(2,1)} custom-call(bf16[3,8,32,1152]{3,2,1,0:T(8,128)(2,1)S(1)} %get-tuple-element.11.win_ref, s32[3,4,128]{2,1,0:T(4,128)S(1)} %get-tuple-element.12.docs_ref, bf16[16,512,256]{2,1,0:T(8,128)(2,1)S(1)} %get-tuple-element.13.qp, bf16[512,2048]{1,0:T(8,128)(2,1)S(1)} %get-tuple-element.14.wk_ref, ...), custom_call_target="tpu_custom_call" | custom-call | tf_op jit(solution)/shard_map/pallas_call | solution.py:429

commit v5 on v4

--- a/solution.py
+++ b/solution.py
@@ -11,7 +11,8 @@
 MESH = pl.DeviceIdType.MESH
 BF16, F32 = jnp.bfloat16, jnp.float32
 HEADS = 16
-GROUP = 4
+UNROLLED = ((1, 512), (0, 256))
+SOME = 2
 T = 256
 BIG = 1e30
 SCALE = math.log2(math.e) / math.sqrt(192)
@@ -35,11 +36,14 @@
     return jnp.transpose(jnp.broadcast_to(row, (128, 128)).astype(F32)).astype(jnp.int32)
 
 
-def key_tail(rope, row):
+def document_mask(row):
     lane = lax.broadcasted_iota(jnp.int32, (128, 128), 1)
     other = (lane >= 64) & (lane < 80) & (documents_down(row) != lane - 64)
-    rope = jnp.concatenate([rope.astype(F32), jnp.zeros((128, 64), F32)], axis=1)
-    return jnp.where(other, -BIG, rope).astype(BF16)
+    return jnp.where(other, -BIG, 0.0).astype(BF16)
+
+
+def key_tail(rope, mask):
+    return jnp.concatenate([rope, mask[:, 64:]], axis=1)
 
 
 def query_tail(row):
@@ -62,7 +66,7 @@
 
 def gather_kernel(lat_ref, docs_ref, q_ref, wk_ref, wv_ref,
                   win, docs_s, qp, wk_s, wv_s, acc_s,
-                  lat_s, own_s, q_s, k_s, v_s, tail_s, qtail_s,
+                  lat_s, own_s, q_s, k_s, v_s, tail_s, qtail_s, mask_s, causal_s,
                   send, recv, relay_send, relay_recv, misc_send, misc_recv, load_sem):
     ctx, dp = lax.axis_index("ctx"), lax.axis_index("dp")
     x, y, core = dp // 2, dp % 2, ctx % 2
@@ -133,6 +137,7 @@
     loads[1].wait()
     for r in range(4):
         qtail_s[pl.ds(128 * r, 128), :] = query_tail(docs_s[2, r:r + 1, :])
+        mask_s[pl.ds(128 * r, 128), :] = document_mask(docs_s[2, r:r + 1, :])
 
     @pl.when(ctx < 2)
     def _():
@@ -169,37 +174,38 @@
 
     lax.fori_loop(0, HEADS // 2, prepare, 0)
 
-    def widen(kinds):
-        latent = rows_of(win.at[2], [shard[k] for k in kinds])
+    sets = ((0, 1, 2, 4), (3, 5, 6, 7))
+
+    def widen(i):
+        latent = rows_of(win.at[2], [shard[k] for k in sets[i]])
+        rope = rope_of(win.at[2], [shard[k] for k in sets[i]])
+        for n, k in enumerate(sets[i]):
+            mask = mask_s[pl.ds(pl.multiple_of(shard[k] * 64, 64), 64), :]
+            tail_s[pl.ds(T * i + 64 * n, 64), :] = key_tail(rope[64 * n:64 * n + 64], mask)
 
         def some(g, carry):
             columns = pl.ds(pl.multiple_of(g * 512, 512), 512)
-            for weight, out in ((wk_s, k_s), (wv_s, v_s)):
-                wide = expand(latent, weight[:, columns])
-                for i, k in enumerate(kinds):
-                    out[pl.ds(pl.multiple_of(shard[k] * 64, 64), 64), columns] = wide[64 * i:64 * i + 64]
+            k_s[pl.ds(T * i, T), columns] = expand(latent, wk_s[:, columns])
+            v_s[pl.ds(T * i, T), columns] = expand(latent, wv_s[:, columns])
             return carry
 
         lax.fori_loop(0, 4, some, 0)
 
-    def own(g, carry):
-        causal = causal_mask()
-        tail = tail_s[...]
-        for h in range(GROUP):
-            head = g * GROUP + h
-            columns = pl.ds(pl.multiple_of(head * 128, 128), 128)
-            keys = jnp.concatenate([k_s[:, columns], tail], axis=1)
-            value = with_ones(v_s[:, columns])
-            for qb in range(2):
-                s = scores(qp[head, pl.ds(qb * T, T), :], keys[:(qb + 1) * T])
-                diagonal = jnp.where(causal, s[:, qb * T:], -BIG)
-                s = diagonal if qb == 0 else jnp.concatenate([s[:, :T], diagonal], axis=1)
-                weights = jnp.exp2(s).astype(BF16)
-                acc_s[head, pl.ds(qb * T, T), :] = jnp.dot(weights, value[:(qb + 1) * T], preferred_element_type=F32)
-        return carry
-
-    def owns(g):
-        lax.fori_loop(g, g + 1, own, 0)
+    def attend(i, start, end):
+        rows = pl.ds(T * i, T)
+
+        def some(g, carry):
+            tail = tail_s[rows, :]
+            for h in range(8):
+                head = g * 8 + h
+                columns = pl.ds(pl.multiple_of(head * 128, 128), 128)
+                keys = jnp.concatenate([k_s[rows, columns], tail], axis=1)
+                weights = jnp.exp2(scores(qp[head], keys) + causal_s[i]).astype(BF16)
+                part = jnp.dot(weights, with_ones(v_s[rows, columns]), preferred_element_type=F32)
+                acc_s[head] = part if i == 0 else acc_s[head] + part
+            return carry
+
+        lax.fori_loop(start, end, some, 0)
 
     forward = (ctx < 14) & jnp.logical_not(before_turn)
 
@@ -214,6 +220,12 @@
 
     def late(k):
         pl.when(turn)(lambda: earlier_shard(k))
+
+    query_at = lax.broadcasted_iota(jnp.int32, (512, 64), 0)
+    ahead = query_at - lax.broadcasted_iota(jnp.int32, (512, 64), 1)
+    for i in range(2):
+        visible = jnp.concatenate([jnp.where(ahead >= shard[k] * 64, 0.0, -BIG) for k in sets[i]], axis=1)
+        causal_s[i] = visible
 
     got(1, 1)
     for where in ("right", "left", "far"):
@@ -228,14 +240,16 @@
     in_time(0)
     loads[3].wait()
     loads[4].wait()
-    widen((0, 1, 2, 4))
+    widen(0)
     late(0)
     for where in ("right", "left", "far"):
         give(0, 0, where, turn)
+    attend(0, 0, 1)
     got(1, 6)
     give(1, 6, "next", forward)
     relay_if(1, 6)
     in_time(2)
+    attend(0, 1, 2)
     got(1, 3)
     relay_if(1, 3)
     got(1, 5)
@@ -243,22 +257,18 @@
     in_time(4)
     got(1, 7)
     relay_if(1, 7)
-    widen((3, 5, 6, 7))
-    for r in range(4):
-        tail_s[pl.ds(128 * r, 128), :] = key_tail(rope_of(win.at[2], (2 * r, 2 * r + 1)), docs_s[2, r:r + 1, :])
+    widen(1)
     late(2)
     late(4)
-    owns(0)
     earlier_shard(6)
-    owns(1)
+    attend(1, 0, 1)
     for k in (1, 3):
         got(0, k)
         relay_if(0, k)
-    owns(2)
+    attend(1, 1, 2)
     for k in (5, 7):
         got(0, k)
         relay_if(0, k)
-    owns(3)
 
     pl.when(ctx >= 1)(d1.wait_recv)
     pl.when(ctx >= 2)(d2.wait_recv)
@@ -301,6 +311,8 @@
             pltpu.VMEM((512, HEADS * 128), BF16),
             pltpu.VMEM((512, 128), BF16),
             pltpu.VMEM((512, 128), BF16),
+            pltpu.VMEM((512, 128), BF16),
+            pltpu.VMEM((2, 512, T), F32),
             pltpu.SemaphoreType.DMA((48,)),
             pltpu.SemaphoreType.DMA((2, 8)),
             pltpu.SemaphoreType.DMA((8,)),
@@ -313,7 +325,9 @@
     )(*operands)
 
 
-def earlier_kernel(win_ref, docs_ref, qp, wk_ref, wv_ref, acc_ref, out_ref, o_s, k_s, v_s, tail_s, rng_s, out_sem):
+def earlier_kernel(win_ref, docs_ref, qp, wk_ref, wv_ref, acc_ref, out_ref, o_s, k_s, v_s, k2_s, v2_s, tail_s, rng_s, out_sem):
+    wide = ((k_s, v_s), (k2_s, v2_s))
+
     def document(row):
         b, rest = divmod(row, 512)
         return docs_ref[b, rest // 128, rest % 128]
@@ -330,47 +344,64 @@
     def tails(start, end):
         for r in range(start, end):
             rope = rope_of(window, (2 * r, 2 * r + 1))
-            tail_s[pl.ds(128 * r, 128), :] = key_tail(rope, docs_ref[r // 4, r % 4:r % 4 + 1, :])
+            tail_s[pl.ds(128 * r, 128), :] = key_tail(rope, document_mask(docs_ref[r // 4, r % 4:r % 4 + 1, :]))
 
     rng_s[0] = jnp.ones((T, 128), F32)
     rng_s[1] = jnp.ones((T, 128), F32)
 
-    def store(g, h, row, acc):
+    def store(head, row, acc):
         total = acc[:, 128:]
-        o_s[g, pl.ds(row, acc.shape[0]), h * 128:(h + 1) * 128] = (acc[:, :128] / total).astype(BF16)
+        o_s[head, pl.ds(row, acc.shape[0]), :] = (acc[:, :128] / total).astype(BF16)
         for t in range(acc.shape[0] // T):
             rng_s[0] = jnp.minimum(rng_s[0], total[t * T:(t + 1) * T])
             rng_s[1] = jnp.maximum(rng_s[1], total[t * T:(t + 1) * T])
 
-    def write(g):
-        return pltpu.make_async_copy(o_s.at[g], out_ref.at[:, pl.ds(pl.multiple_of(g * GROUP * 128, 128), GROUP * 128)], out_sem.at[g])
+    def write(head):
+        return pltpu.make_async_copy(o_s.at[head], out_ref.at[:, pl.ds(pl.multiple_of(head * 128, 128), 128)], out_sem.at[head])
 
     def run(start, reach):
         count = 4 - start
-        if count:
-            tails(2 * start, 8)
-
-        def step(g, carry):
-            columns = pl.ds(pl.multiple_of(g * GROUP * 128, 128), GROUP * 128)
-            if count:
-                latent = rows_of(window, range(4 * start, 16))
-                k_s[pl.ds(0, count * T), :] = expand(latent, wk_ref[:, columns])
-                v_s[pl.ds(0, count * T), :] = expand(latent, wv_ref[:, columns])
-            for h in range(GROUP):
-                head = g * GROUP + h
+        every = pl.ds(0, count * T)
+
+        def widen(head, heads, k, v):
+            part = pl.ds(pl.multiple_of(head * 128, 128), heads * 128)
+            latent = rows_of(window, range(4 * start, 16))
+            k[every, pl.ds(0, heads * 128)] = expand(latent, wk_ref[:, part])
+            v[every, pl.ds(0, heads * 128)] = expand(latent, wv_ref[:, part])
+
+        def attend(first_head, heads, k, v):
+            for h in range(heads):
+                head = first_head + h
+                own = slice(h * 128, h * 128 + 128)
                 acc = acc_ref[head, pl.ds(0, reach), :]
                 for c in range(count):
                     rows = pl.ds(c * T, T)
-                    keys = jnp.concatenate([k_s[rows, h * 128:(h + 1) * 128], tail_s[pl.ds((start + c) * T, T), :]], axis=1)
+                    keys = jnp.concatenate([k[rows, own], tail_s[pl.ds((start + c) * T, T), :]], axis=1)
                     weights = jnp.exp2(scores(qp[head, pl.ds(0, reach), :], keys)).astype(BF16)
-                    acc = acc + jnp.dot(weights, with_ones(v_s[rows, h * 128:(h + 1) * 128]), preferred_element_type=F32)
-                store(g, h, 0, acc)
+                    acc = acc + jnp.dot(weights, with_ones(v[rows, own]), preferred_element_type=F32)
+                store(head, 0, acc)
                 if reach < 512:
-                    store(g, h, reach, acc_ref[head, pl.ds(reach, 512 - reach), :])
-            write(g).start()
-            return carry
-
-        lax.fori_loop(0, HEADS // GROUP, step, 0)
+                    store(head, reach, acc_ref[head, pl.ds(reach, 512 - reach), :])
+                write(head).start()
+
+        if count:
+            tails(2 * start, 8)
+
+        if (start, reach) in UNROLLED:
+            slots = ((k_s, v_s), (k2_s, v2_s))
+            widen(0, SOME, *slots[0])
+            for i in range(HEADS // SOME):
+                if (i + 1) * SOME < HEADS:
+                    widen((i + 1) * SOME, SOME, *slots[(i + 1) % 2])
+                attend(i * SOME, SOME, *slots[i % 2])
+        else:
+            def step(i, carry):
+                if count:
+                    widen(4 * i, 4, k_s, v_s)
+                attend(4 * i, 4, k_s, v_s)
+                return carry
+
+            lax.fori_loop(0, HEADS // 4, step, 0)
 
     for start in range(5):
         for reach in ((512,) if start == 4 else (256,) if start == 0 else (256, 512)):
@@ -378,8 +409,8 @@
             if start < 4:
                 chosen = chosen & (both if reach == 512 else jnp.logical_not(both))
             pl.when(chosen)(functools.partial(run, start, reach))
-    for g in range(HEADS // GROUP):
-        write(g).wait()
+    for head in range(HEADS):
+        write(head).wait()
 
     inside = (jnp.min(rng_s[0]) >= LOW) & (jnp.max(rng_s[1]) <= HIGH)
 
@@ -387,41 +418,41 @@
     def _():
         tails(0, 12)
 
-        def group(g, carry):
-            columns = pl.ds(pl.multiple_of(g * GROUP * 128, 128), GROUP * 128)
+        def one(head, carry):
+            part = pl.ds(pl.multiple_of(head * 128, 128), 128)
+            own = pl.ds(0, 128)
 
             def widen(c, carry):
                 latent = rows_of(window, [4 * c + i for i in range(4)])
                 rows = pl.ds(pl.multiple_of(c * T, T), T)
-                k_s[rows, :] = expand(latent, wk_ref[:, columns])
-                v_s[rows, :] = expand(latent, wv_ref[:, columns])
+                k_s[rows, own] = expand(latent, wk_ref[:, part])
+                v_s[rows, own] = expand(latent, wv_ref[:, part])
                 return carry
 
             lax.fori_loop(first, 6, widen, 0)
             causal = causal_mask()
-            for h in range(GROUP):
-                for qb in range(2):
-                    end = 4 + qb
-
-                    def body(c, state):
-                        peak, acc = state
-                        rows = pl.ds(pl.multiple_of(c * T, T), T)
-                        keys = jnp.concatenate([k_s[rows, h * 128:(h + 1) * 128], tail_s[rows, :]], axis=1)
-                        s = scores(qp[g * GROUP + h, pl.ds(qb * T, T), :], keys)
-                        s = jnp.where(causal | (c < end), s, -BIG)
-                        new = jnp.maximum(peak, jnp.max(s, axis=1, keepdims=True))
-                        weights = jnp.exp2(s - new).astype(BF16)
-                        t = jnp.dot(weights, with_ones(v_s[rows, h * 128:(h + 1) * 128]), preferred_element_type=F32)
-                        return new, acc * jnp.exp2(peak - new) + t
-
-                    initial = (jnp.full((T, 1), -BIG, F32), jnp.zeros((T, 256), F32))
-                    _, acc = lax.fori_loop(first, end + 1, body, initial)
-                    o_s[g, pl.ds(qb * T, T), h * 128:(h + 1) * 128] = (acc[:, :128] / acc[:, 128:]).astype(BF16)
-            write(g).start()
-            write(g).wait()
+            for qb in range(2):
+                end = 4 + qb
+
+                def body(c, state):
+                    peak, acc = state
+                    rows = pl.ds(pl.multiple_of(c * T, T), T)
+                    keys = jnp.concatenate([k_s[rows, own], tail_s[rows, :]], axis=1)
+                    s = scores(qp[head, pl.ds(qb * T, T), :], keys)
+                    s = jnp.where(causal | (c < end), s, -BIG)
+                    new = jnp.maximum(peak, jnp.max(s, axis=1, keepdims=True))
+                    weights = jnp.exp2(s - new).astype(BF16)
+                    t = jnp.dot(weights, with_ones(v_s[rows, own]), preferred_element_type=F32)
+                    return new, acc * jnp.exp2(peak - new) + t
+
+                initial = (jnp.full((T, 1), -BIG, F32), jnp.zeros((T, 256), F32))
+                _, acc = lax.fori_loop(first, end + 1, body, initial)
+                o_s[head, pl.ds(qb * T, T), :] = (acc[:, :128] / acc[:, 128:]).astype(BF16)
+            write(head).start()
+            write(head).wait()
             return carry
 
-        lax.fori_loop(0, HEADS // GROUP, group, 0)
+        lax.fori_loop(0, HEADS, one, 0)
 
 
 def earlier(window, docs, qp, w_key, w_value, acc):
@@ -432,14 +463,16 @@
         in_specs=[vmem] * 6,
         out_specs=hbm,
         scratch_shapes=[
-            pltpu.VMEM((HEADS // GROUP, 512, GROUP * 128), BF16),
-            pltpu.VMEM((1536, GROUP * 128), BF16),
-            pltpu.VMEM((1536, GROUP * 128), BF16),
+            pltpu.VMEM((HEADS, 512, 128), BF16),
+            pltpu.VMEM((1536, 512), BF16),
+            pltpu.VMEM((1536, 512), BF16),
+            pltpu.VMEM((1024, 512), BF16),
+            pltpu.VMEM((1024, 512), BF16),
             pltpu.VMEM((1536, 128), BF16),
             pltpu.VMEM((2, T, 128), F32),
-            pltpu.SemaphoreType.DMA((HEADS // GROUP,)),
+            pltpu.SemaphoreType.DMA((HEADS,)),
         ],
-        compiler_params=pltpu.CompilerParams(vmem_limit_bytes=20 * 2**20),
+        compiler_params=pltpu.CompilerParams(vmem_limit_bytes=26 * 2**20),
     )(window, docs, qp, w_key, w_value, acc)
 
 

time: 132 us -> 155 us (1.17)
  the two profiles are of different devices: /device:TPU:17 before, /device:TPU:113 now
where the time goes in v5:
time: 155 us
  Pallas kernels  155 us (100%)
    pallas_call x1, Pallas kernels, earlier(): pl.pallas_call(earlier_kernel, out_shape=jax.ShapeDtypeStruct((512, 2048)...  137 us
    pallas_call x1, Pallas kernels, gather(): pl.pallas_call(gather_kernel, out_shape=(pltpu.VMEM((3, 8, 32, 1152), BF1...  17.9 us

profile of v5, /device:TPU:113, one launch (start us, length us, event | category | flops | bytes accessed | tf_op | source)
XLA Modules:
  0.0 154.9 jit_solution(12555380928711994646)
XLA Ops:
  0.0 17.9 %shard_map.55 = (bf16[3,8,32,1152]{3,2,1,0:T(8,128)(2,1)S(1)}, s32[3,4,128]{2,1,0:T(4,128)S(1)}, bf16[16,512,256]{2,1,0:T(8,128)(2,1)S(1)}, bf16[512,2048]{1,0:T...) custom-call(bf16[64,576]{1,0:T(8,128)(2,1)} %lat_ref.1, s32[4,128]{1,0:T(4,128)} %bitcast.1, ...), custom_call_target="tpu_custom_call" | custom-call | tf_op jit(solution)/shard_map/pallas_call | solution.py:294
  17.9 136.9 %shard_map.56 = bf16[512,2048]{1,0:T(8,128)(2,1)} custom-call(bf16[3,8,32,1152]{3,2,1,0:T(8,128)(2,1)S(1)} %get-tuple-element.11.win_ref, s32[3,4,128]{2,1,0:T(4,128)S(1)} %get-tuple-element.12.docs_ref, bf16[16,512,256]{2,1,0:T(8,128)(2,1)S(1)} %get-tuple-element.13.qp, bf16[512,2048]{1,0:T(8,128)(2,1)S(1)} %get-tuple-element.14.wk_ref, ...), custom_call_target="tpu_custom_call" | custom-call | tf_op jit(solution)/shard_map/pallas_call | solution.py:460

commit v6 on v5

--- a/solution.py
+++ b/solution.py
@@ -152,11 +152,13 @@
     d1 = remote(docs_ref, docs_s.at[1], misc_send.at[0], misc_recv.at[0], next1)
     d2 = remote(docs_ref, docs_s.at[0], misc_send.at[1], misc_recv.at[1], next2)
 
+    forward = (ctx < 14) & jnp.logical_not(before_turn)
     pl.semaphore_wait(barrier, 4 + jnp.where(ctx < 15, 1, 0) + jnp.where(ctx < 14, 1, 0) + core)
 
+    give(1, 0, "next", before_turn)
     for where in ("partner", "right", "left", "far"):
         give(1, 0, where)
-    give(1, 0, "next", ctx < 14)
+    give(1, 0, "next", forward)
     pl.when(ctx < 14)(d2.start)
     pl.when(ctx < 15)(d1.start)
     relay_if(1, 0)
@@ -207,19 +209,26 @@
 
         lax.fori_loop(start, end, some, 0)
 
-    forward = (ctx < 14) & jnp.logical_not(before_turn)
-
-    def earlier_shard(k):
+    def to_partner(k):
+        return remote(piece(0, k), piece(0, k), send.at[40 + k], recv.at[0, k ^ 1], peers["partner"])
+
+    def earlier_shard(k, pass_on=True):
         pl.when(ctx >= 2)(lambda: got(0, k))
-        c = remote(piece(0, k), piece(0, k), send.at[40 + k], recv.at[0, k ^ 1], peers["partner"])
-        c.start()
+        if pass_on:
+            to_partner(k).start()
         relay_if(0, k)
 
+    straight = jnp.logical_not(turn)
+
     def in_time(k):
-        pl.when(jnp.logical_not(turn))(lambda: earlier_shard(k))
-
-    def late(k):
-        pl.when(turn)(lambda: earlier_shard(k))
+        pl.when(straight)(lambda: earlier_shard(k))
+
+    def late(k, pass_on):
+        pl.when(turn)(lambda: earlier_shard(k, pass_on))
+
+    def partner_shard():
+        got(0, 1)
+        relay_if(0, 1)
 
     query_at = lax.broadcasted_iota(jnp.int32, (512, 64), 0)
     ahead = query_at - lax.broadcasted_iota(jnp.int32, (512, 64), 1)
@@ -241,8 +250,8 @@
     loads[3].wait()
     loads[4].wait()
     widen(0)
-    late(0)
-    for where in ("right", "left", "far"):
+    late(0, True)
+    for where in ("far", "right", "left"):
         give(0, 0, where, turn)
     attend(0, 0, 1)
     got(1, 6)
@@ -257,14 +266,17 @@
     in_time(4)
     got(1, 7)
     relay_if(1, 7)
+    pl.when(turn)(partner_shard)
+    for where in ("right", "left"):
+        give(0, 1, where, turn)
     widen(1)
-    late(2)
-    late(4)
+    late(2, False)
+    late(4, False)
     earlier_shard(6)
     attend(1, 0, 1)
-    for k in (1, 3):
-        got(0, k)
-        relay_if(0, k)
+    pl.when(straight)(partner_shard)
+    got(0, 3)
+    relay_if(0, 3)
     attend(1, 1, 2)
     for k in (5, 7):
         got(0, k)
@@ -280,8 +292,10 @@
             c.wait_send()
         else:
             pl.when(condition)(c.wait_send)
-    for k in (0, 2, 4, 6):
-        remote(piece(0, k), piece(0, k), send.at[40 + k], recv.at[0, k ^ 1], peers["partner"]).wait_send()
+    for k in (0, 6):
+        to_partner(k).wait_send()
+    for k in (2, 4):
+        pl.when(straight)(to_partner(k).wait_send)
     for k in range(8):
         relay(k).wait_send()
     pl.when(ctx < 14)(d2.wait_send)

time: 155 us -> 157 us (1.013)
  the two profiles are of different devices: /device:TPU:113 before, /device:TPU:16 now
where the time goes in v6:
time: 157 us; the launch traced here: 158 us
  Pallas kernels  157 us (100%)
    pallas_call x1, Pallas kernels, earlier(): pl.pallas_call(earlier_kernel, out_shape=jax.ShapeDtypeStruct((512, 2048)...  137 us
    pallas_call x1, Pallas kernels, gather(): pl.pallas_call(gather_kernel, out_shape=(pltpu.VMEM((3, 8, 32, 1152), BF1...  20.5 us

profile of v6, /device:TPU:16, one launch (start us, length us, event | category | flops | bytes accessed | tf_op | source)
XLA Modules:
  0.0 157.6 jit_solution(6627546881268184230)
XLA Ops:
  0.0 20.5 %shard_map.55 = (bf16[3,8,32,1152]{3,2,1,0:T(8,128)(2,1)S(1)}, s32[3,4,128]{2,1,0:T(4,128)S(1)}, bf16[16,512,256]{2,1,0:T(8,128)(2,1)S(1)}, bf16[512,2048]{1,0:T...) custom-call(bf16[64,576]{1,0:T(8,128)(2,1)} %lat_ref.1, s32[4,128]{1,0:T(4,128)} %bitcast.1, ...), custom_call_target="tpu_custom_call" | custom-call | tf_op jit(solution)/shard_map/pallas_call | solution.py:308
  20.5 136.9 %shard_map.56 = bf16[512,2048]{1,0:T(8,128)(2,1)} custom-call(bf16[3,8,32,1152]{3,2,1,0:T(8,128)(2,1)S(1)} %get-tuple-element.11.win_ref, s32[3,4,128]{2,1,0:T(4,128)S(1)} %get-tuple-element.12.docs_ref, bf16[16,512,256]{2,1,0:T(8,128)(2,1)S(1)} %get-tuple-element.13.qp, bf16[512,2048]{1,0:T(8,128)(2,1)S(1)} %get-tuple-element.14.wk_ref, ...), custom_call_target="tpu_custom_call" | custom-call | tf_op jit(solution)/shard_map/pallas_call | solution.py:474
